TPU v7x, 512 devices: a whole 4x8x8 slice. The times are simulated.
512 devices in a mesh: gx: 8 (over z), gy: 8 (over y_hi, core), gz: 8 (over y_lo, x).
Axes of the slice: x: 4, y: 8 (y_hi: 4, y_lo: 2; y = y_hi * 2 + y_lo), z: 8, core: 2. Of those that a mesh axis runs over, the one named last changes fastest.
Arguments:
- source_coefs: float32 [2, 5, 5, 5, 1048576], P(None, None, None, None, ('gx', 'gy', 'gz')), may hold values from -6 to 6
- speed_first: float32 [16, 16, 16], replicated, may hold values from 0.5 to 2
- speed_second: float32 [16, 32, 16], replicated, may hold values from 0.5 to 2
Outputs:
- image_coefs: float32 [2, 5, 5, 5, 1048576], P(None, None, None, None, ('gx', 'gy', 'gz'))
All inputs are finite; a program needn't handle non-finite values.
Results may differ from a plain program's by a relative error of at most 0.00045.
Values sent between devices are 32-bit elements; how exact they have to be, the bound alone decides.
No kernel may reach another device: no remote copies, remote signals or barrier semaphores. Data moves between devices by JAX's collectives and lax.ppermute only.
A program may use at most 64 MiB of HBM per device.

v0:
```python
import math

import jax
import jax.numpy as jnp
import numpy as np
from jax import lax
from jax.sharding import PartitionSpec as P

CHEB = 5
KMAX = 512
TX = 8
TY = 16
TZ = 16


TWO_PI = 2.0 * math.pi


def from_partner(value, axis, stride):
    mask = 2**stride
    pairs = [(source, source ^ mask) for source in range(lax.axis_size(axis))]
    return lax.ppermute(value, axis, pairs)


def chebyshev_points():
    return 0.5 * np.cos(np.pi * np.arange(CHEB) / (CHEB - 1))


def lagrange_tables():
    chebyshev = chebyshev_points()
    tables = np.ones((2, CHEB, CHEB))
    for child_side in range(2):
        shifted = (chebyshev + child_side - 0.5) / 2.0
        for target in range(CHEB):
            for factor in range(CHEB):
                if factor != target:
                    tables[child_side, target, :] *= (shifted - chebyshev[factor]) / (
                        chebyshev[target] - chebyshev[factor]
                    )
    return jnp.asarray(tables, jnp.float32)


def phase_cycles(targets, speeds, grids, center):
    target_x, target_y, target_z = targets
    grid_x, grid_y, grid_z = grids
    delta_x = grid_x - center[0]
    delta_y = grid_y - center[1]
    delta_z = grid_z - center[2]
    along_target = (
        delta_x[:, None, None, None] * target_x
        + delta_y[None, :, None, None] * target_y
        + delta_z[None, None, :, None] * target_z
    )
    numerator = (
        (delta_x * (grid_x + center[0]))[:, None, None]
        + (delta_y * (grid_y + center[1]))[None, :, None]
        + (delta_z * (grid_z + center[2]))[None, None, :]
    )
    radius = jnp.sqrt(
        (grid_x * grid_x)[:, None, None]
        + (grid_y * grid_y)[None, :, None]
        + (grid_z * grid_z)[None, None, :]
    )
    radius = radius + jnp.sqrt(
        center[0] * center[0] + center[1] * center[1] + center[2] * center[2]
    )
    return along_target + speeds * (numerator / radius)[..., None]


def box_grids(center, widths, merge_dim, child_side):
    chebyshev = jnp.asarray(chebyshev_points(), jnp.float32)
    grids = [center[dim_index] + widths[dim_index] * chebyshev for dim_index in range(3)]
    if merge_dim >= 0:
        offset = child_side.astype(jnp.float32) - 0.5
        grids[merge_dim] = center[merge_dim] + widths[merge_dim] * (chebyshev + offset) * 0.5
    return grids


def child_term(stacked, child_side, merge_dim, targets, speeds, center, widths):
    grids = box_grids(center, widths, merge_dim, child_side)
    angle = TWO_PI * phase_cycles(targets, speeds, grids, center)
    cosine = jnp.cos(angle)
    sine = jnp.sin(angle)
    turned = jnp.stack(
        [stacked[0] * cosine + stacked[1] * sine, stacked[1] * cosine - stacked[0] * sine]
    )
    tables = lagrange_tables()
    table = jnp.where(child_side == 0, tables[0], tables[1])
    if merge_dim == 0:
        return jnp.einsum("pm,cmqrn->cpqrn", table, turned, precision=lax.Precision.HIGHEST)
    return jnp.einsum("qm,cpmrn->cpqrn", table, turned, precision=lax.Precision.HIGHEST)


def finish(total, targets, speeds, center, widths):
    grids = box_grids(center, widths, -1, None)
    angle = TWO_PI * phase_cycles(targets, speeds, grids, center)
    cosine = jnp.cos(angle)
    sine = jnp.sin(angle)
    return jnp.stack([total[0] * cosine - total[1] * sine, total[0] * sine + total[1] * cosine])


def target_boxes(count, first_side, second_side):
    box_order = jnp.arange(count, dtype=jnp.int32)
    along_x = box_order // (TY * TZ)
    along_y = box_order // TZ % TY
    along_z = box_order % TZ
    target_x = ((2 * along_x + first_side).astype(jnp.float32) + 0.5) / (2.0 * TX)
    if second_side is None:
        target_y = (along_y.astype(jnp.float32) + 0.5) / TY
    else:
        target_y = ((2 * along_y + second_side).astype(jnp.float32) + 0.5) / (2.0 * TY)
    target_z = (along_z.astype(jnp.float32) + 0.5) / TZ
    return (target_x, target_y, target_z)


def first_speeds(speed_first, first_side):
    shaped = speed_first.reshape(TX, 2, TY, TZ)
    return lax.dynamic_index_in_dim(shaped, first_side, 1, keepdims=False).reshape(-1)


def second_speeds(speed_second, first_side, second_side):
    shaped = speed_second.reshape(TX, 2, TY, 2, TZ)
    picked = lax.dynamic_index_in_dim(shaped, first_side, 1, keepdims=False)
    return lax.dynamic_index_in_dim(picked, second_side, 2, keepdims=False).reshape(-1)


def shards(source_coefs, speed_first, speed_second):
    count = source_coefs.shape[-1]
    width_x = KMAX // lax.axis_size("gx")
    width_y = KMAX // lax.axis_size("gy")
    width_z = KMAX // lax.axis_size("gz")
    half_x = lax.axis_size("gx") // 2
    half_y = lax.axis_size("gy") // 2
    bit_first = (lax.axis_size("gx") * lax.axis_size("gy") * lax.axis_size("gz")).bit_length() - 2
    bit_second = (lax.axis_size("gy") * lax.axis_size("gz")).bit_length() - 2
    index_x = lax.axis_index("gx")
    index_y = lax.axis_index("gy")
    index_z = lax.axis_index("gz")
    side_x = index_x // half_x
    side_y = index_y // half_y
    box_y = 2 * (index_y % half_y) + side_y
    center_one = (
        ((2 * (index_x % half_x) + 1) * width_x).astype(jnp.float32),
        (box_y.astype(jnp.float32) + 0.5) * width_y,
        (index_z.astype(jnp.float32) + 0.5) * width_z,
    )
    widths_one = (2.0 * width_x, 1.0 * width_y, 1.0 * width_z)
    targets_own = target_boxes(count, side_x, None)
    speeds_own = first_speeds(speed_first, side_x)
    targets_far = target_boxes(count, 1 - side_x, None)
    speeds_far = first_speeds(speed_first, 1 - side_x)
    mine = child_term(source_coefs, side_x, 0, targets_own, speeds_own, center_one, widths_one)
    theirs = child_term(source_coefs, side_x, 0, targets_far, speeds_far, center_one, widths_one)
    total_one = mine + from_partner(theirs, ("gx", "gy", "gz"), bit_first)
    level_one = finish(total_one, targets_own, speeds_own, center_one, widths_one)
    center_two = (
        center_one[0],
        ((2 * (index_y % half_y) + 1) * width_y).astype(jnp.float32),
        center_one[2],
    )
    widths_two = (2.0 * width_x, 2.0 * width_y, 1.0 * width_z)
    targets_kept = target_boxes(count, side_x, side_y)
    speeds_kept = second_speeds(speed_second, side_x, side_y)
    targets_other = target_boxes(count, side_x, 1 - side_y)
    speeds_other = second_speeds(speed_second, side_x, 1 - side_y)
    mine_two = child_term(level_one, side_y, 1, targets_kept, speeds_kept, center_two, widths_two)
    theirs_two = child_term(
        level_one, side_y, 1, targets_other, speeds_other, center_two, widths_two
    )
    total_two = mine_two + from_partner(theirs_two, ("gx", "gy", "gz"), bit_second)
    return finish(total_two, targets_kept, speeds_kept, center_two, widths_two)


def solution(mesh):
    in_specs = (P(None, None, None, None, ("gx", "gy", "gz")), P(), P())
    out_specs = P(None, None, None, None, ("gx", "gy", "gz"))
    return jax.shard_map(shards, mesh=mesh, in_specs=in_specs, out_specs=out_specs, check_vma=False)
```

profile of v0, /device:TPU:100, one launch (start us, length us, event | category | flops | bytes accessed | tf_op | source)
XLA Modules:
  0.0 274.8 jit_solution(4013487758623593496)
XLA Ops:
  0.1 0.9 constant_dynamic-slice_fusion.1
  1.0 0.1 mul.913
  1.1 0.1 mul.942
  1.3 0.0 copy-start.10
  1.3 0.0 copy-start.8
  1.3 0.0 copy-start.9
  1.3 4.3 %fusion.78 = (f32[1,5,5,5,2048]{4,0,3,2,1:T(1,128)S(1)}, f32[1,5,5,5,2048]{4,0,3,2,1:T(1,128)S(1)}) fusion(f32[2,5,5,5,2048]{4,0,3,2,1:T(2,128)} %param.13), kind=kLoop, calls=%fused_computation.161 | loop fusion | bytes 4096000 | tf_op jit(solution)/shard_map/slice | solution.py:85
  5.6 0.0 copy-done.10
  5.6 0.0 copy-done.8
  5.7 0.0 copy-done.9
  5.7 0.1 broadcast_multiply_fusion
  5.8 0.1 broadcast_multiply_fusion.7
  5.9 0.1 broadcast_multiply_fusion.5
  5.9 0.1 broadcast_add_fusion.7
  6.0 0.1 broadcast_add_fusion.6
  6.1 1.1 broadcast_add_fusion
  7.2 0.1 add_divide_fusion
  7.3 0.0 copy-start.5
  7.3 0.0 copy-start.6
  7.3 13.1 %fusion.20 = (f32[1,5,5,5,2048]{4,1,3,2,0:T(8,128)S(1)}, f32[1,5,5,5,2048]{4,1,3,2,0:T(8,128)S(1)}, f32[1,5,5,5,2048]{4,1,3,2,0:T(8,128)S(1)}, f32[1,5,5,5,2048]{4,1,3,2,0:T(8,128)S(1)}) fusion(f32[1,5,5,5,2048]{4,0,3,2,1:T(1,128)S(1)} %get-tuple-element.22, f32[1,5,5,5,2048]{4,0,3,2,1:T(1,128)S(1)} %get-tuple-element.21, ...), kind=kLoop, calls=%fused_computation.27 | loop fusion | flops 5120000 | bytes 6611444 | tf_op jit(solution)/shard_map/add | solution.py:85
  20.4 0.0 copy-done.5
  20.4 0.0 copy-done.6
  20.4 3.8 %fusion.12 = f32[2,5,5,5,2048]{4,1,3,2,0:T(8,128)S(1)} fusion(f32[1,5,5,5,2048]{4,1,3,2,0:T(8,128)S(1)} %get-tuple-element.19, f32[1,5,5,5,2048]{4,1,3,2,0:T(8,128)S(1)} %get-tuple-element.20, f32[1,5,5]{2,1,0:T(8,128)S(1)} %copy-done.5, f32[1,5,5]{2,1,0:T(8,128)S(1)} %copy-done.6, pred[]{:T(512)S(6)} %eq.21), kind=kOutput, calls=%fused_computation.17 | convolution fusion | flops 31232024 | bytes 4096201 | tf_op jit(solution)/shard_map/pm,cmqrn->cpqrn/dot_general | solution.py:90
  24.3 0.0 copy-start.4
  24.3 2.9 %copy.31 = f32[2,5,5,5,2048]{4,0,3,2,1:T(2,128)} copy(f32[2,5,5,5,2048]{4,1,3,2,0:T(8,128)S(1)} %fusion.12) | data formatting | bytes 4096000 | tf_op jit(solution)/shard_map/pm,cmqrn->cpqrn/transpose | solution.py:90
  27.2 10.4 %collective-permute-start = (f32[2,5,5,5,2048]{4,0,3,2,1:T(2,128)}, f32[2,5,5,5,2048]{4,0,3,2,1:T(2,128)}, u32[]{:S(2)}, u32[]{:S(2)}) collective-permute-start(f32[2,5,5,5,2048]{4,0,3,2,1:T(2,128)} %copy.31), channel_id=1, source_target_pairs={{0,256},{1,257},{2,258},{3,259},{4,260},{5,261},{6,262},{7,263},{8... | collective-permute-start | bytes 6144008 | tf_op jit(solution)/shard_map/ppermute | solution.py:22
  37.6 0.8 copy.33
  38.5 1.4 dynamic-slice_reduce_fusion.1
  39.8 0.1 mul.988
  39.9 0.1 mul.1016
  40.0 86.5 %collective-permute-done = f32[2,5,5,5,2048]{4,0,3,2,1:T(2,128)} collective-permute-done((f32[2,5,5,5,2048]{4,0,3,2,1:T(2,128)}, f32[2,5,5,5,2048]{4,0,3,2,1:T(2,128)}, u32[]{:S(2)}, u32[]{:S(2)}) %collective-permute-start) | collective-permute-done | bytes 2048032 | tf_op jit(solution)/shard_map/ppermute | solution.py:22
  126.6 7.2 %bitcast_add_fusion.1 = f32[2,5,5,5,2048]{4,1,3,2,0:T(8,128)S(1)} fusion(f32[2,5,5,5,2048]{4,0,3,2,1:T(2,128)} %collective-permute-done, f32[1,5,5,5,2048]{4,1,3,2,0:T(8,128)S(1)} %get-tuple-element.16, f32[1,5,5,5,2048]{4,1,3,2,0:T(8,128)S(1)} %get-tuple-element.15, f32[1,5,5]{2,1,0:T(8,128)S(1)} %copy-done.5, f32[1,5,5]{2,1,0:T(8,128)} %constant.244, ...), kind=kOutput, calls=%fused_computation.12 | convolution fusion | flops 31744024 | bytes 6144201 | tf_op jit(solution)/shard_map/pm,cmqrn->cpqrn/dot_general | solution.py:90
  133.8 12.5 %multiply_add_fusion.2 = (f32[1,5,5,5,2048]{4,1,3,2,0:T(8,128)S(1)}, f32[1,5,5,5,2048]{4,1,3,2,0:T(8,128)S(1)}, f32[1,5,5,5,2048]{4,1,3,2,0:T(8,128)S(1)}) fusion(f32[5,5,5]{0,2,1:T(8,128)S(1)} %get-tuple-element.38, f32[2048]{0:T(1024)S(1)} %mul.988, f32[5,5,2048]{2,0,1:T(8,128)S(1)} %copy-done, f32[5,2048]{1,0:T(8,128)S(1)} %get-tuple-element.73, ...), kind=kLoop, calls=%fused_computation.42 | loop fusion | flops 4352000 | bytes 5587944 | tf_op jit(solution)/shard_map/add | solution.py:85
  146.3 12.6 %multiply_add_fusion.1 = (f32[1,5,5,5,2048]{4,1,3,2,0:T(8,128)S(1)}, f32[1,5,5,5,2048]{4,1,3,2,0:T(8,128)S(1)}, f32[1,5,5,5,2048]{4,1,3,2,0:T(8,128)S(1)}) fusion(f32[1,5,5,5,2048]{4,1,3,2,0:T(8,128)S(1)} %get-tuple-element.8, f32[1,5,5,5,2048]{4,1,3,2,0:T(8,128)S(1)} %get-tuple-element.9, f32[2048]{0:T(1024)S(1)} %mul.1016, f32[5,5,2048]{2,0,1:T(8,128)S(1)} %copy-done.2, ...), kind=kLoop, calls=%fused_computation.37 | loop fusion | flops 4352000 | bytes 5587444 | tf_op jit(solution)/shard_map/add | solution.py:85
  158.9 0.0 copy-start.7
  158.9 0.4 pad_maximum_fusion.1
  159.3 0.3 copy-done.7
  159.6 4.9 %fusion.17 = f32[2,5,5,5,2048]{4,2,3,1,0:T(8,128)S(1)} fusion(f32[2,5,5,5,2048]{4,1,3,2,0:T(8,128)S(1)} %pad_maximum_fusion.1, f32[1,5,5]{2,1,0:T(8,128)S(1)} %copy-done.5, f32[1,5,5]{2,1,0:T(8,128)S(1)} %copy-done.7, pred[]{:T(512)S(6)} %eq.22), kind=kOutput, calls=%fused_computation.18 | convolution fusion | flops 30720024 | bytes 4096201 | tf_op jit(solution)/shard_map/qm,cpmrn->cpqrn/dot_general | solution.py:91
  164.5 1.6 copy.37
  166.1 2.2 collective-permute-start.1
  168.4 0.3 pad_maximum_fusion
  168.7 4.9 %fusion.10 = f32[2,5,5,2048,5]{3,4,2,1,0:T(8,128)S(1)} fusion(f32[2,5,5,5,2048]{4,1,3,2,0:T(8,128)S(1)} %pad_maximum_fusion, f32[1,5,5]{2,1,0:T(8,128)S(1)} %copy-done.5, f32[1,5,5]{2,1,0:T(8,128)S(1)} %copy-done.7, pred[]{:T(512)S(6)} %eq.22), kind=kOutput, calls=%fused_computation.15 | convolution fusion | flops 30720024 | bytes 4096201 | tf_op jit(solution)/shard_map/qm,cpmrn->cpqrn/dot_general | solution.py:91
  173.6 0.0 copy-start.1
  173.6 88.7 %collective-permute-done.1 = f32[2,5,5,5,2048]{4,0,3,2,1:T(2,128)S(1)} collective-permute-done((f32[2,5,5,5,2048]{4,0,3,2,1:T(2,128)S(1)}, f32[2,5,5,5,2048]{4,0,3,2,1:T(2,128)S(1)}, u32[]{:S(2)}, u32[]{:S(2)}) %collective-permute-start.1) | collective-permute-done | bytes 2048032 | tf_op jit(solution)/shard_map/ppermute | solution.py:22
  262.3 2.3 bitcast_add_fusion
  264.6 6.6 %multiply_subtract_fusion = (f32[1,5,5,5,2048]{4,1,3,2,0:T(8,128)S(1)}, f32[1,5,5,5,2048]{4,1,3,2,0:T(8,128)S(1)}) fusion(f32[2,5,5,5,2048]{4,1,3,2,0:T(8,128)S(1)} %bitcast_add_fusion, f32[5,5,5]{0,2,1:T(8,128)S(1)} %get-tuple-element.35, f32[5,5,2048]{2,0,1:T(8,128)S(1)} %copy-done.1, f32[2048]{0:T(1024)S(1)} %mul.988, f32[5,2048]{1,0:T(8,128)S(1)} %get-tuple-element.73), kind=kLoop, calls=%fused_computation.32 | loop fusion | flops 2560000 | bytes 4350452 | tf_op jit(solution)/shard_map/sub | solution.py:99
  271.3 0.4 pad_maximum_fusion.2
  271.6 2.9 %copy.39 = f32[2,5,5,5,2048]{4,0,3,2,1:T(2,128)} copy(f32[2,5,5,5,2048]{4,1,3,2,0:T(8,128)S(1)} %pad_maximum_fusion.2) | data formatting | bytes 4096000 | tf_op jit(solution)/shard_map/stack | solution.py:99
  (14 shorter events, 0.1 us)
Async XLA Ops:
  1.3 4.3 %copy-start.10 = (f32[5]{0:T(128)S(1)}, f32[5]{0:T(128)}, u32[]{:S(2)}) copy-start(f32[5]{0:T(128)} %constant.242) | copy-start | bytes 64
  1.3 4.4 %copy-start.8 = (f32[5]{0:T(128)S(1)}, f32[5]{0:T(128)}, u32[]{:S(2)}) copy-start(f32[5]{0:T(128)} %constant.240.clone) | copy-start | bytes 64
  1.3 4.4 %copy-start.9 = (f32[5]{0:T(128)S(1)}, f32[5]{0:T(128)}, u32[]{:S(2)}) copy-start(f32[5]{0:T(128)} %constant.245) | copy-start | bytes 64
  7.3 13.1 %copy-start.5 = (f32[1,5,5]{2,1,0:T(8,128)S(1)}, f32[1,5,5]{2,1,0:T(8,128)}, u32[]{:S(2)}) copy-start(f32[1,5,5]{2,1,0:T(8,128)} %constant.243) | copy-start | bytes 304
  7.3 13.1 %copy-start.6 = (f32[1,5,5]{2,1,0:T(8,128)S(1)}, f32[1,5,5]{2,1,0:T(8,128)}, u32[]{:S(2)}) copy-start(f32[1,5,5]{2,1,0:T(8,128)} %constant.244) | copy-start | bytes 304
  24.3 13.3 %copy-start.4 = (f32[16,32,16]{1,2,0:T(8,128)S(1)}, f32[16,32,16]{1,2,0:T(8,128)}, u32[]{:S(2)}) copy-start(f32[16,32,16]{1,2,0:T(8,128)} %param.15) | copy-start | bytes 98308
  27.2 99.4 %collective-permute-start = (f32[2,5,5,5,2048]{4,0,3,2,1:T(2,128)}, f32[2,5,5,5,2048]{4,0,3,2,1:T(2,128)}, u32[]{:S(2)}, u32[]{:S(2)}) collective-permute-start(f32[2,5,5,5,2048]{4,0,3,2,1:T(2,128)} %copy.31), channel_id=1, source_target_pairs={{0,256},{1,257},{2,258},{3,259},{4,260},{5,261},{6,262},{7,263},{8... | collective-permute-start | bytes 6144008 | tf_op jit(solution)/shard_map/ppermute | solution.py:22
  126.5 7.2 %copy-start = (f32[5,5,2048]{2,0,1:T(8,128)S(1)}, f32[5,5,2048]{2,0,1:T(8,128)}, u32[]{:S(2)}) copy-start(f32[5,5,2048]{2,0,1:T(8,128)} %get-tuple-element.26) | copy-start | bytes 614404
  126.6 7.2 %copy-start.3 = (f32[5,5,2048]{2,0,1:T(8,128)S(1)}, f32[5,5,2048]{2,0,1:T(8,128)}, u32[]{:S(2)}) copy-start(f32[5,5,2048]{2,0,1:T(8,128)} %get-tuple-element.28) | copy-start | bytes 614404
  133.8 12.6 %copy-start.2 = (f32[5,5,2048]{2,0,1:T(8,128)S(1)}, f32[5,5,2048]{2,0,1:T(8,128)}, u32[]{:S(2)}) copy-start(f32[5,5,2048]{2,0,1:T(8,128)} %get-tuple-element.27) | copy-start | bytes 614404
  158.9 0.7 copy-start.7
  166.1 96.2 %collective-permute-start.1 = (f32[2,5,5,5,2048]{4,0,3,2,1:T(2,128)S(1)}, f32[2,5,5,5,2048]{4,0,3,2,1:T(2,128)S(1)}, u32[]{:S(2)}, u32[]{:S(2)}) collective-permute-start(f32[2,5,5,5,2048]{4,0,3,2,1:T(2,128)S(1)} %copy.37), channel_id=1, source_target_pairs={{0,32},{1,33},{2,34},{3,35},{4,36},{5,37},{6,38},{7,39},{8,40},{9,... | collective-permute-start | bytes 6144008 | tf_op jit(solution)/shard_map/ppermute | solution.py:22
  173.6 91.0 %copy-start.1 = (f32[5,5,2048]{2,0,1:T(8,128)S(1)}, f32[5,5,2048]{2,0,1:T(8,128)}, u32[]{:S(2)}) copy-start(f32[5,5,2048]{2,0,1:T(8,128)} %get-tuple-element.25) | copy-start | bytes 614404
where the time goes:
time: 278 us; the launch traced here: 275 us
  waiting for transfers between devices  175 us (63%)
  other arithmetic  49.9 us (18%)
  matrix products  20.8 us (7%)
  local copies, waits for them, and re-layouts  15.4 us (6%)
  starting transfers between devices  12.6 us (5%)
    ppermute x2, waiting for transfers between devices, from_partner(): return lax.ppermute(value, axis, pairs)  175 us
    add x3, other arithmetic, child_term(): stacked[0] * cosine + stacked[1] * sine  38.2 us
    ppermute x2, starting transfers between devices, from_partner(): return lax.ppermute(value, axis, pairs)  12.6 us
    dot_general x2, matrix products, child_term(): jnp.einsum('pm,cmqrn->cpqrn', table, turned, precision=lax.Precision.HIGH...  11 us
    dot_general x2, matrix products, child_term(): jnp.einsum('qm,cpmrn->cpqrn', table, turned, precision=lax.Precision.HIGH...  9.82 us
    sub x1, other arithmetic, finish(): total[0] * cosine - total[1] * sine  6.64 us
  transfers between devices with their start and end apart: 2, of which 2 were waited for; matrix products, arithmetic and copies ran while one was open for 3% of the time, Pallas kernels for 0%

commit v1 on v0

v1 whole, which is shorter than its diff:
```python
import functools

import jax
import jax.numpy as jnp
import numpy as np
from jax import lax
from jax.experimental import pallas as pl
from jax.experimental.pallas import tpu as pltpu
from jax.sharding import PartitionSpec as P

CHEB = 5
KMAX = 512
TX = 8
TY = 16
TZ = 16
ROWS = 8
LANES = 128
AXES = ("gx", "gy", "gz")
PIECES = ((0, 3), (3, 2))
ROUNDER = 1.5 * 2.0**23
SINE = (4.442867903031852, -7.307443421308049, 3.594788078718595, -0.784374031470659)
COSINE = (
    1.41421349656502,
    -6.978850988239763,
    5.739461170697818,
    -1.8835629874053614,
    0.3106981920186687,
)

POINTS = 0.5 * np.cos(np.pi * np.arange(CHEB) / (CHEB - 1))
POINTS[CHEB // 2] = 0.0


def lagrange_table():
    shifted = (POINTS - 0.5) / 2.0
    table = np.ones((CHEB, CHEB))
    for target in range(CHEB):
        for factor in range(CHEB):
            if factor != target:
                table[target] *= (shifted - POINTS[factor]) / (POINTS[target] - POINTS[factor])
    return table


TABLE = lagrange_table()


def from_partner(value, stride):
    mask = 2**stride
    pairs = [(source, source ^ mask) for source in range(lax.axis_size(AXES))]
    return lax.ppermute(value, AXES, pairs)


def fraction(cycles):
    return cycles - ((cycles + ROUNDER) - ROUNDER)


def turn(cycles):
    part = fraction(cycles)
    square = part * part
    sine = SINE[-1] * square + SINE[-2]
    for factor in SINE[-3::-1]:
        sine = sine * square + factor
    sine = sine * part
    cosine = COSINE[-1] * square + COSINE[-2]
    for factor in COSINE[-3::-1]:
        cosine = cosine * square + factor
    return 1.0 - sine * sine, sine * cosine


def forward(value, cycles):
    cosine, sine = turn(cycles)
    return value[0] * cosine - value[1] * sine, value[0] * sine + value[1] * cosine


def backward(value, cycles):
    cosine, sine = turn(cycles)
    return value[0] * cosine + value[1] * sine, value[1] * cosine - value[0] * sine


def merge(values):
    merged = []
    for target in range(CHEB):
        parts = []
        for part in range(2):
            total = float(TABLE[target, 1]) * values[1][part]
            for point in (2, 3):
                total = total + float(TABLE[target, point]) * values[point][part]
            if target == 2:
                total = total + values[0][part]
            if target == 4:
                total = total + values[4][part]
            parts.append(total)
        merged.append(tuple(parts))
    return merged


def flipped(first, second):
    return [
        (a[0] + b[0], a[1] + b[1]) for a, b in zip(first, second[::-1], strict=True)
    ]


class Targets:
    def __init__(self, half, table, sides, speeds):
        row = lax.broadcasted_iota(jnp.int32, (ROWS, LANES), 0) + ROWS * half
        lane = lax.broadcasted_iota(jnp.int32, (ROWS, LANES), 1)
        self.along_x = lax.shift_right_logical(row, 1).astype(jnp.float32)
        self.along_y = (
            lax.bitwise_and(row, 1) * 8 + lax.shift_right_logical(lane, 4)
        ).astype(jnp.float32)
        self.along_z = lax.bitwise_and(lane, 15).astype(jnp.float32)
        self.z = (self.along_z + 0.5) / TZ
        self.y = (self.along_y + 0.5) / TY
        self.table = table
        self.side_x, self.side_y = sides[0], sides[1]
        self.sign_x = 1.0 - 2.0 * self.side_x.astype(jnp.float32)
        self.sign_y = 1.0 - 2.0 * self.side_y.astype(jnp.float32)
        self.speeds = [speeds[k, ROWS * half : ROWS * (half + 1), :] for k in range(5)]

    def x(self, far):
        side = self.side_x.astype(jnp.float32)
        side = 1.0 - side if far else side
        return (2.0 * self.along_x + side + 0.5) / (2.0 * TX)

    def fine_y(self, far):
        side = self.side_y.astype(jnp.float32)
        side = 1.0 - side if far else side
        return (2.0 * self.along_y + side + 0.5) / (2.0 * TY)

    def point(self, index):
        return self.table[8, index]

    def radius(self, which, p, q, r):
        return self.table[which, p * (CHEB * CHEB) + q * CHEB + r]


def end(side, index):
    return index + side * (CHEB - 1 - 2 * index)


def first_merge(at, weights, which, sign_x, sign_y, flips, x, speed, q, r, r_local):
    flip_x, flip_y = flips
    rows = at.point(q) * (64.0 * sign_y) * at.y + at.point(r) * 64.0 * at.z
    rows = fraction(rows)
    turned = []
    for m in range(CHEB):
        cycles = (x[m] + rows) + speed * at.radius(which, m, q, r)
        point = (end(flip_x, m), end(flip_y, q), r_local)
        value = (
            weights[(*point, pl.ds(0, ROWS, stride=2), slice(None))],
            weights[(*point, pl.ds(1, ROWS, stride=2), slice(None))],
        )
        turned.append(backward(value, cycles))
    return merge(turned)


def first_x(sign, x):
    return [fraction((sign * (64.0 * float(z - 0.5))) * x) for z in POINTS]


def between_y(at, sign, fine):
    return [
        fraction(sign * (float(64.0 * z) * at.y - float(64.0 * (z - 0.5)) * fine)) for z in POINTS
    ]


def second_merge(at, level, tables, between, speeds, p, r, r_local):
    turned = []
    for q in range(CHEB):
        cycles = (
            between[q]
            + speeds[0] * at.radius(tables[0], p, q, r)
            - speeds[1] * at.radius(tables[1], p, q, r)
        )
        turned.append(forward((level[p, q, r_local, 0], level[p, q, r_local, 1]), cycles))
    return merge(turned)


def put(ref, values, *place):
    ref[(*place, 0)] = values[0]
    ref[(*place, 1)] = values[1]


def level_kernel(first, count, table, sides, speeds, own, got, level, send):
    at = Targets(0, table, sides, speeds)
    x = at.x(False)
    x_own, x_got = first_x(at.sign_x, x), first_x(-at.sign_x, x)

    def one_level(q, carry):
        for k in range(count):
            mine = first_merge(
                at, own, 0, at.sign_x, at.sign_y, (at.side_x, at.side_y), x_own, at.speeds[0], q, first + k, k
            )
            theirs = first_merge(
                at, got, 1, -at.sign_x, at.sign_y, (1 - at.side_x, at.side_y), x_got, at.speeds[0], q, first + k, k
            )
            for p, value in enumerate(flipped(mine, theirs)):
                put(level, value, p, q, k)
        return carry

    lax.fori_loop(0, CHEB, one_level, 0)
    between = between_y(at, at.sign_y, at.fine_y(True))

    def two_level(p, carry):
        for k in range(count):
            shares = second_merge(
                at, level, (3, 5), between, (at.speeds[0], at.speeds[3]), p, first + k, k
            )
            for q, value in enumerate(shares):
                put(send, value, p, q, k)
        return carry

    lax.fori_loop(0, CHEB, two_level, 0)


def both_kernel(first, count, far, table, sides, speeds, own, got, send, level_own, level_got):
    at = Targets(1, table, sides, speeds)
    x = first_x(at.sign_x, at.x(far))
    speed, speed_two = at.speeds[int(far)], at.speeds[4 if far else 2]

    def one_level(q, carry):
        for k in range(count):
            for weights, which, sign_y, flip_y, level in (
                (own, 0, at.sign_y, at.side_y, level_own),
                (got, 2, -at.sign_y, 1 - at.side_y, level_got),
            ):
                merged = first_merge(
                    at, weights, which, at.sign_x, sign_y, (at.side_x, flip_y), x, speed, q, first + k, k
                )
                for p, value in enumerate(merged):
                    put(level, value, p, q, k)
        return carry

    lax.fori_loop(0, CHEB, one_level, 0)
    fine = at.fine_y(False)
    between_own, between_got = between_y(at, at.sign_y, fine), between_y(at, -at.sign_y, fine)

    def two_level(p, carry):
        for k in range(count):
            mine = second_merge(at, level_own, (3, 5), between_own, (speed, speed_two), p, first + k, k)
            theirs = second_merge(at, level_got, (4, 6), between_got, (speed, speed_two), p, first + k, k)
            for q, value in enumerate(flipped(mine, theirs)):
                put(send, value, p, q, k)
        return carry

    lax.fori_loop(0, CHEB, two_level, 0)


def last_kernel(half, first, table, sides, speeds, level, got, *rest):
    out = rest[-1]
    at = Targets(half, table, sides, speeds)
    r = first + pl.program_id(0)
    x, fine = at.x(False), at.fine_y(False)
    along_y = [fraction((at.sign_y * float(128.0 * z)) * fine) for z in POINTS]
    along_z = fraction(at.point(r) * 64.0 * at.z)
    along_yz = [value + along_z for value in along_y]
    between = between_y(at, at.sign_y, fine)

    def one_p(p, carry):
        along_x = fraction((at.sign_x * 128.0 * at.point(p)) * x)
        if half == 0:
            mine = second_merge(
                at, level, (3, 5), between, (at.speeds[0], at.speeds[2]), p, r, 0
            )
        for q in range(CHEB):
            if half == 0:
                value = mine[q]
                other = (got[p, CHEB - 1 - q, 0, 0], got[p, CHEB - 1 - q, 0, 1])
            else:
                value = (level[p, q, 0, 0], level[p, q, 0, 1])
                other = (got[CHEB - 1 - p, q, 0, 0], got[CHEB - 1 - p, q, 0, 1])
            cycles = (along_x + along_yz[q]) + at.speeds[2] * at.radius(7, p, q, r)
            value = forward((value[0] + other[0], value[1] + other[1]), cycles)
            point = (end(at.side_x, p), end(at.side_y, q), 0)
            out[(*point, pl.ds(0, ROWS, stride=2), slice(None))] = value[0]
            out[(*point, pl.ds(1, ROWS, stride=2), slice(None))] = value[1]
        return carry

    lax.fori_loop(0, CHEB, one_p, 0)


SMEM = pl.BlockSpec(memory_space=pltpu.SMEM)
VMEM = pl.BlockSpec(memory_space=pltpu.VMEM)


def complex_shape(count):
    return (CHEB, CHEB, count, 2, ROWS, LANES)


def cost(sets):
    return pl.CostEstimate(flops=sets * ROWS * LANES * 60, bytes_accessed=sets * 20000, transcendentals=0)


def run_level(first, count, facts, own, got):
    shape = jax.ShapeDtypeStruct(complex_shape(count), jnp.float32)
    return pl.pallas_call(
        functools.partial(level_kernel, first, count),
        in_specs=[SMEM, SMEM, VMEM, VMEM, VMEM],
        out_specs=[VMEM, VMEM],
        out_shape=[shape, shape],
        cost_estimate=cost(75 * count),
        name=f"level_{first}",
    )(*facts, own, got)


def run_both(first, count, far, facts, own, got):
    return pl.pallas_call(
        functools.partial(both_kernel, first, count, far),
        in_specs=[SMEM, SMEM, VMEM, VMEM, VMEM],
        out_specs=VMEM,
        out_shape=jax.ShapeDtypeStruct(complex_shape(count), jnp.float32),
        scratch_shapes=[pltpu.VMEM(complex_shape(count), jnp.float32)] * 2,
        cost_estimate=cost(100 * count),
        name=f"both_{first}_{int(far)}",
    )(*facts, own, got)


def run_last(half, first, count, facts, level, got, out):
    block = (CHEB, CHEB, 1, 2, ROWS, LANES)
    in_specs = [SMEM, SMEM, VMEM] + [pl.BlockSpec(block, lambda i: (0, 0, i, 0, 0, 0))] * 2
    operands = [*facts, level, got]
    aliases = {}
    if out is not None:
        in_specs.append(pl.BlockSpec(memory_space=pl.ANY))
        operands.append(out)
        aliases = {5: 0}
    return pl.pallas_call(
        functools.partial(last_kernel, half, first),
        grid=(count,),
        in_specs=in_specs,
        out_specs=pl.BlockSpec(
            (CHEB, CHEB, 1, 2 * ROWS, LANES), lambda i: (0, 0, first + i, half, 0)
        ),
        out_shape=jax.ShapeDtypeStruct((CHEB, CHEB, CHEB, 4 * ROWS, LANES), jnp.float32),
        input_output_aliases=aliases,
        cost_estimate=cost(50 * count),
        name=f"last_{half}_{first}",
    )(*operands)


def device_facts(speed_first, speed_second):
    width = [KMAX // lax.axis_size(axis) for axis in AXES]
    half_x, half_y = lax.axis_size("gx") // 2, lax.axis_size("gy") // 2
    index_x, index_y, index_z = (lax.axis_index(axis) for axis in AXES)
    side_x, side_y = index_x // half_x, index_y // half_y
    sign_x = 1.0 - 2.0 * side_x.astype(jnp.float32)
    sign_y = 1.0 - 2.0 * side_y.astype(jnp.float32)
    box_y = (2 * (index_y % half_y)).astype(jnp.float32) * width[1]
    center_x = ((2 * (index_x % half_x) + 1) * width[0]).astype(jnp.float32)
    center_z = (index_z.astype(jnp.float32) + 0.5) * width[2]
    own_y = box_y + (side_y.astype(jnp.float32) + 0.5) * width[1]
    far_y = box_y + (1.5 - side_y.astype(jnp.float32)) * width[1]
    middle_y = box_y + width[1]

    index = np.arange(LANES)
    inside = index < CHEB**3
    points = [
        np.where(inside, POINTS[index // step % CHEB], 0.0).astype(np.float32)
        for step in (CHEB * CHEB, CHEB, 1)
    ]
    child_x = sign_x * (width[0] * (points[0] - np.float32(0.5)))
    parent_x = sign_x * (2.0 * width[0] * points[0])
    child_y = sign_y * (width[1] * points[1])
    parent_y = sign_y * (2.0 * width[1] * points[1])
    pairs = (
        (child_x, own_y, child_y, own_y),
        (-child_x, own_y, child_y, own_y),
        (child_x, far_y, -child_y, far_y),
        (parent_x, own_y, child_y, own_y),
        (parent_x, far_y, -child_y, far_y),
        (parent_x, own_y, child_y, middle_y),
        (parent_x, far_y, -child_y, middle_y),
        (parent_x, middle_y, parent_y, middle_y),
    )
    grid_x = center_x + jnp.stack([pair[0] for pair in pairs])
    grid_y = jnp.stack([pair[1] + pair[2] for pair in pairs])
    center_y = jnp.stack([pair[3] for pair in pairs])[:, None]
    offset_z = (width[2] * points[2])[None]
    grid_z = center_z + offset_z
    numerator = (
        (grid_x - center_x) * (grid_x + center_x)
        + (grid_y - center_y) * (grid_y + center_y)
        + offset_z * (grid_z + center_z)
    )
    radius = jnp.sqrt(grid_x * grid_x + grid_y * grid_y + grid_z * grid_z) + jnp.sqrt(
        center_x * center_x + center_y * center_y + center_z * center_z
    )
    last = np.zeros((8, LANES), np.float32)
    last[0, :CHEB] = POINTS
    table = jnp.concatenate([numerator / radius, last], 0)
    sides = jnp.stack([side_x, side_y]).astype(jnp.int32)

    first = speed_first.reshape(TX, 2, TY * TZ)
    first_own = jnp.where(side_x == 0, first[:, 0], first[:, 1])
    first_far = jnp.where(side_x == 0, first[:, 1], first[:, 0])
    second = speed_second.reshape(TX, 2, TY, 2, TZ)
    second_own = jnp.where(side_x == 0, second[:, 0], second[:, 1])
    second_far = jnp.where(side_x == 0, second[:, 1], second[:, 0])
    speeds = [
        first_own,
        first_far,
        jnp.where(side_y == 0, second_own[:, :, 0], second_own[:, :, 1]),
        jnp.where(side_y == 0, second_own[:, :, 1], second_own[:, :, 0]),
        jnp.where(side_y == 0, second_far[:, :, 0], second_far[:, :, 1]),
    ]
    return table, sides, jnp.stack([speed.reshape(2 * ROWS, LANES) for speed in speeds])


def shards(source_coefs, speed_first, speed_second):
    bit_first = (lax.axis_size("gx") * lax.axis_size("gy") * lax.axis_size("gz")).bit_length() - 2
    bit_second = (lax.axis_size("gy") * lax.axis_size("gz")).bit_length() - 2
    weights = source_coefs.reshape(2, CHEB, CHEB, CHEB, 2 * ROWS, LANES)
    weights = weights.transpose(1, 2, 3, 4, 0, 5).reshape(CHEB, CHEB, CHEB, 4 * ROWS, LANES)
    raw = [
        [weights[:, :, first : first + count, 16 * half : 16 * (half + 1)] for first, count in PIECES]
        for half in range(2)
    ]
    got = [[], []]
    for k in range(len(PIECES)):
        got[0].append(from_partner(raw[0][k], bit_first))
        got[1].append(from_partner(raw[1][k], bit_second))
    facts = device_facts(speed_first, speed_second)
    levels, shares, arrived, arrived_two = [], [], [], []
    for k, (first, count) in enumerate(PIECES):
        level, send = run_level(first, count, facts, raw[0][k], got[0][k])
        levels.append(level)
        arrived.append(from_partner(send, bit_second))
        send = run_both(first, count, True, facts, raw[1][k], got[1][k])
        arrived_two.append(from_partner(send, bit_first))
        shares.append(run_both(first, count, False, facts, raw[1][k], got[1][k]))
    out = None
    for k, (first, count) in enumerate(PIECES):
        out = run_last(0, first, count, facts, levels[k], arrived[k], out)
        out = run_last(1, first, count, facts, shares[k], arrived_two[k], out)
    out = out.reshape(CHEB, CHEB, CHEB, 2 * ROWS, 2, LANES).transpose(4, 0, 1, 2, 3, 5)
    return out.reshape(source_coefs.shape)


def solution(mesh):
    in_specs = (P(None, None, None, None, ("gx", "gy", "gz")), P(), P())
    out_specs = P(None, None, None, None, ("gx", "gy", "gz"))
    return jax.shard_map(shards, mesh=mesh, in_specs=in_specs, out_specs=out_specs, check_vma=False)
```

time: 278 us -> 118 us (0.42)
  the two profiles are of different devices: /device:TPU:100 before, /device:TPU:21 now
where the time goes in v1:
time: 118 us; the launch traced here: 117 us
  waiting for transfers between devices  37.5 us (32%)
  Pallas kernels  33.5 us (28%)
  starting transfers between devices  33.4 us (28%)
  local copies, waits for them, and re-layouts  9.01 us (8%)
  other arithmetic  3.72 us (3%)
    ppermute x8, waiting for transfers between devices, from_partner(): return lax.ppermute(value, AXES, pairs)  37.5 us
    ppermute x8, starting transfers between devices, from_partner(): return lax.ppermute(value, AXES, pairs)  33.4 us
    pallas_call x4, Pallas kernels, run_both(): pl.pallas_call(functools.partial(both_kernel, first, count, far), in_spec...  14.8 us
    pallas_call x4, Pallas kernels, run_last(): pl.pallas_call(functools.partial(last_kernel, half, first), grid=(count,)...  11.7 us
    pallas_call x2, Pallas kernels, run_level(): pl.pallas_call(functools.partial(level_kernel, first, count), in_specs=[S...  7.01 us
    unnamed x41, local copies, waits for them, and re-layouts  5 us
    slice x2, local copies, waits for them, and re-layouts, shards(): weights[:, :, first:first + count, 16 * half:16 * (half + 1)]  2.59 us
  transfers between devices with their start and end apart: 8, of which 5 were waited for; matrix products, arithmetic and copies ran while one was open for 6% of the time, Pallas kernels for 27%

profile of v1, /device:TPU:21, one launch (start us, length us, event | category | flops | bytes accessed | tf_op | source)
XLA Modules:
  0.0 117.5 jit_solution(10675696703049883603)
XLA Ops:
  0.0 1.4 %fusion.12 = (f32[5,5,3,16,128]{4,3,2,1,0:T(8,128)S(1)}, f32[5,5,3,16,128]{4,3,2,1,0:T(8,128)S(1)}) fusion(f32[5,5,5,32,128]{4,3,2,1,0:T(8,128)} %bitcast.54), kind=kLoop, calls=%fused_computation.36 | loop fusion | bytes 2457600 | tf_op jit(solution)/shard_map/slice | solution.py:415
  1.4 0.0 copy-start.17
  1.4 0.0 copy-start.16
  1.5 0.0 copy-start.13
  1.5 0.0 copy-start.14
  1.5 0.0 copy-start.12
  1.5 10.8 %collective-permute-start.6 = (f32[5,5,3,16,128]{4,3,2,1,0:T(8,128)S(1)}, f32[5,5,3,16,128]{4,3,2,1,0:T(8,128)}, u32[]{:S(2)}, u32[]{:S(2)}) collective-permute-start(f32[5,5,3,16,128]{4,3,2,1,0:T(8,128)S(1)} %get-tuple-element.15.own), channel_id=1, source_target_pairs={{0,256},{1,257},{2,258},{3,259},{4,260},{5,261},{6,262},{7,263},{8... | collective-permute-start | bytes 1843208 | tf_op jit(solution)/shard_map/ppermute | solution.py:50
  12.3 5.7 %collective-permute-start.4 = (f32[5,5,3,16,128]{4,3,2,1,0:T(8,128)S(1)}, f32[5,5,3,16,128]{4,3,2,1,0:T(8,128)S(1)}, u32[]{:S(2)}, u32[]{:S(2)}) collective-permute-start(f32[5,5,3,16,128]{4,3,2,1,0:T(8,128)S(1)} %get-tuple-element.16.own), channel_id=1, source_target_pairs={{0,32},{1,33},{2,34},{3,35},{4,36},{5,37},{6,38},{7,39},{8,40},{9,... | collective-permute-start | bytes 1843208 | tf_op jit(solution)/shard_map/ppermute | solution.py:50
  17.9 1.2 %fusion.13 = (f32[5,5,2,16,128]{4,3,2,1,0:T(8,128)S(1)}, f32[5,5,2,16,128]{4,3,2,1,0:T(8,128)S(1)}) fusion(f32[5,5,5,32,128]{4,3,2,1,0:T(8,128)} %bitcast.55), kind=kLoop, calls=%fused_computation.37 | loop fusion | bytes 1638400 | tf_op jit(solution)/shard_map/slice | solution.py:415
  19.2 1.9 %collective-permute-start.2 = (f32[5,5,2,16,128]{4,3,2,1,0:T(8,128)S(1)}, f32[5,5,2,16,128]{4,3,2,1,0:T(8,128)}, u32[]{:S(2)}, u32[]{:S(2)}) collective-permute-start(f32[5,5,2,16,128]{4,3,2,1,0:T(8,128)S(1)} %get-tuple-element.17.own), channel_id=1, source_target_pairs={{0,256},{1,257},{2,258},{3,259},{4,260},{5,261},{6,262},{7,263},{8... | collective-permute-start | bytes 1228808 | tf_op jit(solution)/shard_map/ppermute | solution.py:50
  21.1 3.5 %collective-permute-start = (f32[5,5,2,16,128]{4,3,2,1,0:T(8,128)S(1)}, f32[5,5,2,16,128]{4,3,2,1,0:T(8,128)S(1)}, u32[]{:S(2)}, u32[]{:S(2)}) collective-permute-start(f32[5,5,2,16,128]{4,3,2,1,0:T(8,128)S(1)} %get-tuple-element.18.own), channel_id=1, source_target_pairs={{0,32},{1,33},{2,34},{3,35},{4,36},{5,37},{6,38},{7,39},{8,40},{9,... | collective-permute-start | bytes 1228808 | tf_op jit(solution)/shard_map/ppermute | solution.py:50
  24.7 0.1 copy.21
  24.8 0.1 fusion
  24.9 0.7 fusion.1
  25.6 1.6 %fusion.3 = (f32[8,16,16]{2,1,0:T(8,128)S(1)}, f32[8,16,16]{2,1,0:T(8,128)S(1)}, f32[8,16,16]{2,1,0:T(8,128)S(1)}) fusion(pred[]{:T(512)S(6)} %eq.8, f32[8,16,2,16]{3,2,1,0:T(2,128)} %fusion.1, f32[8,16,2,16]{3,2,1,0:T(2,128)S(1)} %fusion), kind=kLoop, calls=%fused_computation.8 | loop fusion | flops 6144 | bytes 57345 | tf_op jit(solution)/shard_map/jit(_where)/select_n | solution.py:403
  27.2 0.1 select_n.128
  27.3 1.0 reshape.190
  28.4 0.1 select_n.130
  28.5 0.1 stack.74
  28.7 0.1 select_n.134
  28.9 0.1 add_divide_fusion
  28.9 0.6 pad_add_fusion.sides
  29.5 0.6 pad_maximum_fusion.table
  30.1 3.9 %level_0.1 = (f32[5,5,3,2,8,128]{5,4,3,2,1,0:T(8,128)}, f32[5,5,3,2,8,128]{5,4,3,2,1,0:T(8,128)}) custom-call(f32[16,128]{1,0:T(8,128)} %pad_maximum_fusion.table, s32[2]{0:T(128)} %pad_add_fusion.sides, f32[5,16,128]{2,1,0:T(8,128)} %copy-done.1, f32[5,5,3,16,128]{4,3,2,1,0:T(8,128)} %copy-done.4, f32[5,5,3,16,128]{4,3,2,1,0:T(8,128)} %collective-permute-done.6.got), custom_call_target="tpu_custom_call" | custom-call | flops 13824000 | bytes 4500000 | tf_op jit(solution)/shard_map/level_0/pallas_call | solution.py:296
  34.0 5.6 %collective-permute-start.7 = (f32[5,5,3,2,8,128]{5,4,3,2,1,0:T(8,128)}, f32[5,5,3,2,8,128]{5,4,3,2,1,0:T(8,128)S(1)}, u32[]{:S(2)}, u32[]{:S(2)}) collective-permute-start(f32[5,5,3,2,8,128]{5,4,3,2,1,0:T(8,128)} %get-tuple-element.12), channel_id=1, source_target_pairs={{0,32},{1,33},{2,34},{3,35},{4,36},{5,37},{6,38},{7,39},{8,40},{9,... | collective-permute-start | bytes 1843208 | tf_op jit(solution)/shard_map/ppermute | solution.py:50
  39.6 17.3 %collective-permute-done.4.got = f32[5,5,3,16,128]{4,3,2,1,0:T(8,128)S(1)} collective-permute-done((f32[5,5,3,16,128]{4,3,2,1,0:T(8,128)S(1)}, f32[5,5,3,16,128]{4,3,2,1,0:T(8,128)S(1)}, u32[]{:S(2)}, u32[]{:S(2)}) %collective-permute-start.4) | collective-permute-done | bytes 614432 | tf_op jit(solution)/shard_map/ppermute | solution.py:50
  56.9 0.8 copy-done.3
  57.8 4.1 %both_0_1.1 = f32[5,5,3,2,8,128]{5,4,3,2,1,0:T(8,128)} custom-call(f32[16,128]{1,0:T(8,128)} %pad_maximum_fusion.table, s32[2]{0:T(128)} %pad_add_fusion.sides, f32[5,16,128]{2,1,0:T(8,128)} %copy-done.1, f32[5,5,3,16,128]{4,3,2,1,0:T(8,128)} %copy-done, f32[5,5,3,16,128]{4,3,2,1,0:T(8,128)} %copy-done.3), custom_call_target="tpu_custom_call" | custom-call | flops 18432000 | bytes 6000000 | tf_op jit(solution)/shard_map/both_0_1/pallas_call | solution.py:307
  61.9 2.0 %collective-permute-start.5 = (f32[5,5,3,2,8,128]{5,4,3,2,1,0:T(8,128)}, f32[5,5,3,2,8,128]{5,4,3,2,1,0:T(8,128)S(1)}, u32[]{:S(2)}, u32[]{:S(2)}) collective-permute-start(f32[5,5,3,2,8,128]{5,4,3,2,1,0:T(8,128)} %both_0_1.1), channel_id=1, source_target_pairs={{0,256},{1,257},{2,258},{3,259},{4,260},{5,261},{6,262},{7,263},{8... | collective-permute-start | bytes 1843208 | tf_op jit(solution)/shard_map/ppermute | solution.py:50
  63.9 3.1 %level_3.1 = (f32[5,5,2,2,8,128]{5,4,3,2,1,0:T(8,128)}, f32[5,5,2,2,8,128]{5,4,3,2,1,0:T(8,128)}) custom-call(f32[16,128]{1,0:T(8,128)} %pad_maximum_fusion.table, s32[2]{0:T(128)} %pad_add_fusion.sides, f32[5,16,128]{2,1,0:T(8,128)} %copy-done.1, f32[5,5,2,16,128]{4,3,2,1,0:T(8,128)} %copy-done.6, f32[5,5,2,16,128]{4,3,2,1,0:T(8,128)} %collective-permute-done.2.got), custom_call_target="tpu_custom_call" | custom-call | flops 9216000 | bytes 3000000 | tf_op jit(solution)/shard_map/level_3/pallas_call | solution.py:296
  67.1 1.9 %collective-permute-start.3 = (f32[5,5,2,2,8,128]{5,4,3,2,1,0:T(8,128)}, f32[5,5,2,2,8,128]{5,4,3,2,1,0:T(8,128)S(1)}, u32[]{:S(2)}, u32[]{:S(2)}) collective-permute-start(f32[5,5,2,2,8,128]{5,4,3,2,1,0:T(8,128)} %get-tuple-element.10), channel_id=1, source_target_pairs={{0,32},{1,33},{2,34},{3,35},{4,36},{5,37},{6,38},{7,39},{8,40},{9,... | collective-permute-start | bytes 1228808 | tf_op jit(solution)/shard_map/ppermute | solution.py:50
  69.0 8.4 %collective-permute-done.got = f32[5,5,2,16,128]{4,3,2,1,0:T(8,128)S(1)} collective-permute-done((f32[5,5,2,16,128]{4,3,2,1,0:T(8,128)S(1)}, f32[5,5,2,16,128]{4,3,2,1,0:T(8,128)S(1)}, u32[]{:S(2)}, u32[]{:S(2)}) %collective-permute-start) | collective-permute-done | bytes 409632 | tf_op jit(solution)/shard_map/ppermute | solution.py:50
  77.4 0.8 copy-done.5
  78.2 3.3 %both_3_1.1 = f32[5,5,2,2,8,128]{5,4,3,2,1,0:T(8,128)} custom-call(f32[16,128]{1,0:T(8,128)} %pad_maximum_fusion.table, s32[2]{0:T(128)} %pad_add_fusion.sides, f32[5,16,128]{2,1,0:T(8,128)} %copy-done.1, f32[5,5,2,16,128]{4,3,2,1,0:T(8,128)} %copy-done.2, f32[5,5,2,16,128]{4,3,2,1,0:T(8,128)} %copy-done.5), custom_call_target="tpu_custom_call" | custom-call | flops 12288000 | bytes 4000000 | tf_op jit(solution)/shard_map/both_3_1/pallas_call | solution.py:307
  81.5 1.9 %collective-permute-start.1 = (f32[5,5,2,2,8,128]{5,4,3,2,1,0:T(8,128)}, f32[5,5,2,2,8,128]{5,4,3,2,1,0:T(8,128)S(1)}, u32[]{:S(2)}, u32[]{:S(2)}) collective-permute-start(f32[5,5,2,2,8,128]{5,4,3,2,1,0:T(8,128)} %both_3_1.1), channel_id=1, source_target_pairs={{0,256},{1,257},{2,258},{3,259},{4,260},{5,261},{6,262},{7,263},{8... | collective-permute-start | bytes 1228808 | tf_op jit(solution)/shard_map/ppermute | solution.py:50
  83.4 3.3 %both_3_0.1.level = f32[5,5,2,2,8,128]{5,4,3,2,1,0:T(8,128)} custom-call(f32[16,128]{1,0:T(8,128)} %pad_maximum_fusion.table, s32[2]{0:T(128)} %pad_add_fusion.sides, f32[5,16,128]{2,1,0:T(8,128)} %copy-done.1, f32[5,5,2,16,128]{4,3,2,1,0:T(8,128)} %copy-done.2, f32[5,5,2,16,128]{4,3,2,1,0:T(8,128)} %copy-done.5), custom_call_target="tpu_custom_call" | custom-call | flops 12288000 | bytes 4000000 | tf_op jit(solution)/shard_map/both_3_0/pallas_call | solution.py:307
  86.7 4.1 %both_0_0.1.level = f32[5,5,3,2,8,128]{5,4,3,2,1,0:T(8,128)} custom-call(f32[16,128]{1,0:T(8,128)} %pad_maximum_fusion.table, s32[2]{0:T(128)} %pad_add_fusion.sides, f32[5,16,128]{2,1,0:T(8,128)} %copy-done.1, f32[5,5,3,16,128]{4,3,2,1,0:T(8,128)} %copy-done, f32[5,5,3,16,128]{4,3,2,1,0:T(8,128)} %copy-done.3), custom_call_target="tpu_custom_call" | custom-call | flops 18432000 | bytes 6000000 | tf_op jit(solution)/shard_map/both_0_0/pallas_call | solution.py:307
  90.8 9.1 %collective-permute-done.7.got = f32[5,5,3,2,8,128]{5,4,3,2,1,0:T(8,128)S(1)} collective-permute-done((f32[5,5,3,2,8,128]{5,4,3,2,1,0:T(8,128)}, f32[5,5,3,2,8,128]{5,4,3,2,1,0:T(8,128)S(1)}, u32[]{:S(2)}, u32[]{:S(2)}) %collective-permute-start.7) | collective-permute-done | bytes 614432 | tf_op jit(solution)/shard_map/ppermute | solution.py:50
  100.0 0.8 copy-done.7
  100.8 3.6 %last_0_0.1.rest_0_ = f32[5,5,5,32,128]{4,3,2,1,0:T(8,128)} custom-call(f32[16,128]{1,0:T(8,128)} %pad_maximum_fusion.table, s32[2]{0:T(128)} %pad_add_fusion.sides, f32[5,16,128]{2,1,0:T(8,128)} %copy-done.1, f32[5,5,3,2,8,128]{5,4,3,2,1,0:T(8,128)} %get-tuple-element.11.level, f32[5,5,3,2,8,128]{5,4,3,2,1,0:T(8,128)} %copy-done.7), custom_call_target="tpu_custom_call" | custom-call | flops 9216000 | bytes 3000000 | tf_op jit(solution)/shard_map/last_0_0/pallas_call | solution.py:327
  104.4 0.8 copy-done.8
  105.3 3.3 %last_1_0.1.rest_0_ = f32[5,5,5,32,128]{4,3,2,1,0:T(8,128)} custom-call(f32[16,128]{1,0:T(8,128)} %pad_maximum_fusion.table, s32[2]{0:T(128)} %pad_add_fusion.sides, f32[5,16,128]{2,1,0:T(8,128)} %copy-done.1, f32[5,5,3,2,8,128]{5,4,3,2,1,0:T(8,128)} %both_0_0.1.level, f32[5,5,3,2,8,128]{5,4,3,2,1,0:T(8,128)} %copy-done.8, ...), custom_call_target="tpu_custom_call", output_to_operand_aliasing={{}: (5, {})} | custom-call | flops 9216000 | bytes 3000000 | tf_op jit(solution)/shard_map/last_1_0/pallas_call | solution.py:327
  108.6 0.3 collective-permute-done.3.got
  108.8 0.8 copy-done.10
  109.6 2.5 %last_0_3.1.rest_0_ = f32[5,5,5,32,128]{4,3,2,1,0:T(8,128)} custom-call(f32[16,128]{1,0:T(8,128)} %pad_maximum_fusion.table, s32[2]{0:T(128)} %pad_add_fusion.sides, f32[5,16,128]{2,1,0:T(8,128)} %copy-done.1, f32[5,5,2,2,8,128]{5,4,3,2,1,0:T(8,128)} %get-tuple-element.9.level, f32[5,5,2,2,8,128]{5,4,3,2,1,0:T(8,128)} %copy-done.10, ...), custom_call_target="tpu_custom_call", output_to_operand_aliasing={{}: (5, {})} | custom-call | flops 6144000 | bytes 2000000 | tf_op jit(solution)/shard_map/last_0_3/pallas_call | solution.py:327
  112.1 2.4 %collective-permute-done.1.got = f32[5,5,2,2,8,128]{5,4,3,2,1,0:T(8,128)S(1)} collective-permute-done((f32[5,5,2,2,8,128]{5,4,3,2,1,0:T(8,128)}, f32[5,5,2,2,8,128]{5,4,3,2,1,0:T(8,128)S(1)}, u32[]{:S(2)}, u32[]{:S(2)}) %collective-permute-start.1) | collective-permute-done | bytes 409632 | tf_op jit(solution)/shard_map/ppermute | solution.py:50
  114.5 0.8 copy-done.9
  115.2 2.2 %last_1_3.1 = f32[5,5,5,32,128]{4,3,2,1,0:T(8,128)} custom-call(f32[16,128]{1,0:T(8,128)} %pad_maximum_fusion.table, s32[2]{0:T(128)} %pad_add_fusion.sides, f32[5,16,128]{2,1,0:T(8,128)} %copy-done.1, f32[5,5,2,2,8,128]{5,4,3,2,1,0:T(8,128)} %both_3_0.1.level, f32[5,5,2,2,8,128]{5,4,3,2,1,0:T(8,128)} %copy-done.9, ...), custom_call_target="tpu_custom_call", output_to_operand_aliasing={{}: (5, {})} | custom-call | flops 6144000 | bytes 2000000 | tf_op jit(solution)/shard_map/last_1_3/pallas_call | solution.py:327
  (43 shorter events, 0.2 us)
Async XLA Ops:
  0.0 24.7 %copy-start.11 = (f32[16,32,16]{1,2,0:T(8,128)S(1)}, f32[16,32,16]{1,2,0:T(8,128)}, u32[]{:S(2)}) copy-start(f32[16,32,16]{1,2,0:T(8,128)} %param.11) | copy-start | bytes 98308
  1.4 28.7 %copy-start.4 = (f32[5,5,3,16,128]{4,3,2,1,0:T(8,128)}, f32[5,5,3,16,128]{4,3,2,1,0:T(8,128)S(1)}, u32[]{:S(2)}) copy-start(f32[5,5,3,16,128]{4,3,2,1,0:T(8,128)S(1)} %get-tuple-element.15.own) | copy-start | bytes 1843204
  1.4 32.6 %copy-start = (f32[5,5,3,16,128]{4,3,2,1,0:T(8,128)}, f32[5,5,3,16,128]{4,3,2,1,0:T(8,128)S(1)}, u32[]{:S(2)}) copy-start(f32[5,5,3,16,128]{4,3,2,1,0:T(8,128)S(1)} %get-tuple-element.16.own) | copy-start | bytes 1843204
  1.4 27.1 %copy-start.17 = (f32[1,128]{1,0:T(1,128)S(1)}, f32[1,128]{1,0:T(1,128)}, u32[]{:S(2)}) copy-start(f32[1,128]{1,0:T(1,128)} %constant.81.clone) | copy-start | bytes 1540
  1.4 27.2 %copy-start.15 = (f32[128]{0:T(128)S(1)}, f32[128]{0:T(128)}, u32[]{:S(2)}) copy-start(f32[128]{0:T(128)} %constant.77.clone) | copy-start | bytes 1540
  1.4 27.2 %copy-start.16 = (f32[128]{0:T(128)S(1)}, f32[128]{0:T(128)}, u32[]{:S(2)}) copy-start(f32[128]{0:T(128)} %constant.78.clone) | copy-start | bytes 1540
  1.5 27.2 %copy-start.13 = (f32[128]{0:T(128)S(1)}, f32[128]{0:T(128)}, u32[]{:S(2)}) copy-start(f32[128]{0:T(128)} %constant.79.clone) | copy-start | bytes 1540
  1.5 27.2 %copy-start.14 = (f32[128]{0:T(128)S(1)}, f32[128]{0:T(128)}, u32[]{:S(2)}) copy-start(f32[128]{0:T(128)} %constant.80.clone) | copy-start | bytes 1540
  1.5 28.0 %copy-start.12 = (f32[8,128]{1,0:T(8,128)S(1)}, f32[8,128]{1,0:T(8,128)}, u32[]{:S(2)}) copy-start(f32[8,128]{1,0:T(8,128)} %constant.82.clone) | copy-start | bytes 12292
  1.5 28.6 %collective-permute-start.6 = (f32[5,5,3,16,128]{4,3,2,1,0:T(8,128)S(1)}, f32[5,5,3,16,128]{4,3,2,1,0:T(8,128)}, u32[]{:S(2)}, u32[]{:S(2)}) collective-permute-start(f32[5,5,3,16,128]{4,3,2,1,0:T(8,128)S(1)} %get-tuple-element.15.own), channel_id=1, source_target_pairs={{0,256},{1,257},{2,258},{3,259},{4,260},{5,261},{6,262},{7,263},{8... | collective-permute-start | bytes 1843208 | tf_op jit(solution)/shard_map/ppermute | solution.py:50
  12.3 44.7 %collective-permute-start.4 = (f32[5,5,3,16,128]{4,3,2,1,0:T(8,128)S(1)}, f32[5,5,3,16,128]{4,3,2,1,0:T(8,128)S(1)}, u32[]{:S(2)}, u32[]{:S(2)}) collective-permute-start(f32[5,5,3,16,128]{4,3,2,1,0:T(8,128)S(1)} %get-tuple-element.16.own), channel_id=1, source_target_pairs={{0,32},{1,33},{2,34},{3,35},{4,36},{5,37},{6,38},{7,39},{8,40},{9,... | collective-permute-start | bytes 1843208 | tf_op jit(solution)/shard_map/ppermute | solution.py:50
  19.1 42.7 %copy-start.2 = (f32[5,5,2,16,128]{4,3,2,1,0:T(8,128)}, f32[5,5,2,16,128]{4,3,2,1,0:T(8,128)S(1)}, u32[]{:S(2)}) copy-start(f32[5,5,2,16,128]{4,3,2,1,0:T(8,128)S(1)} %get-tuple-element.18.own) | copy-start | bytes 1228804
  19.2 42.7 %copy-start.6 = (f32[5,5,2,16,128]{4,3,2,1,0:T(8,128)}, f32[5,5,2,16,128]{4,3,2,1,0:T(8,128)S(1)}, u32[]{:S(2)}) copy-start(f32[5,5,2,16,128]{4,3,2,1,0:T(8,128)S(1)} %get-tuple-element.17.own) | copy-start | bytes 1228804
  19.2 44.8 %collective-permute-start.2 = (f32[5,5,2,16,128]{4,3,2,1,0:T(8,128)S(1)}, f32[5,5,2,16,128]{4,3,2,1,0:T(8,128)}, u32[]{:S(2)}, u32[]{:S(2)}) collective-permute-start(f32[5,5,2,16,128]{4,3,2,1,0:T(8,128)S(1)} %get-tuple-element.17.own), channel_id=1, source_target_pairs={{0,256},{1,257},{2,258},{3,259},{4,260},{5,261},{6,262},{7,263},{8... | collective-permute-start | bytes 1228808 | tf_op jit(solution)/shard_map/ppermute | solution.py:50
  21.1 56.3 %collective-permute-start = (f32[5,5,2,16,128]{4,3,2,1,0:T(8,128)S(1)}, f32[5,5,2,16,128]{4,3,2,1,0:T(8,128)S(1)}, u32[]{:S(2)}, u32[]{:S(2)}) collective-permute-start(f32[5,5,2,16,128]{4,3,2,1,0:T(8,128)S(1)} %get-tuple-element.18.own), channel_id=1, source_target_pairs={{0,32},{1,33},{2,34},{3,35},{4,36},{5,37},{6,38},{7,39},{8,40},{9,... | collective-permute-start | bytes 1228808 | tf_op jit(solution)/shard_map/ppermute | solution.py:50
  28.9 1.3 %copy-start.1 = (f32[5,16,128]{2,1,0:T(8,128)}, f32[5,16,128]{2,1,0:T(8,128)S(1)}, u32[]{:S(2)}) copy-start(f32[5,16,128]{2,1,0:T(8,128)S(1)} %constant_dynamic-update-slice_fusion.speeds) | copy-start | bytes 122884
  34.0 66.0 %collective-permute-start.7 = (f32[5,5,3,2,8,128]{5,4,3,2,1,0:T(8,128)}, f32[5,5,3,2,8,128]{5,4,3,2,1,0:T(8,128)S(1)}, u32[]{:S(2)}, u32[]{:S(2)}) collective-permute-start(f32[5,5,3,2,8,128]{5,4,3,2,1,0:T(8,128)} %get-tuple-element.12), channel_id=1, source_target_pairs={{0,32},{1,33},{2,34},{3,35},{4,36},{5,37},{6,38},{7,39},{8,40},{9,... | collective-permute-start | bytes 1843208 | tf_op jit(solution)/shard_map/ppermute | solution.py:50
  56.9 0.8 copy-start.3
  61.9 42.5 %collective-permute-start.5 = (f32[5,5,3,2,8,128]{5,4,3,2,1,0:T(8,128)}, f32[5,5,3,2,8,128]{5,4,3,2,1,0:T(8,128)S(1)}, u32[]{:S(2)}, u32[]{:S(2)}) collective-permute-start(f32[5,5,3,2,8,128]{5,4,3,2,1,0:T(8,128)} %both_0_1.1), channel_id=1, source_target_pairs={{0,256},{1,257},{2,258},{3,259},{4,260},{5,261},{6,262},{7,263},{8... | collective-permute-start | bytes 1843208 | tf_op jit(solution)/shard_map/ppermute | solution.py:50
  67.1 41.8 %collective-permute-start.3 = (f32[5,5,2,2,8,128]{5,4,3,2,1,0:T(8,128)}, f32[5,5,2,2,8,128]{5,4,3,2,1,0:T(8,128)S(1)}, u32[]{:S(2)}, u32[]{:S(2)}) collective-permute-start(f32[5,5,2,2,8,128]{5,4,3,2,1,0:T(8,128)} %get-tuple-element.10), channel_id=1, source_target_pairs={{0,32},{1,33},{2,34},{3,35},{4,36},{5,37},{6,38},{7,39},{8,40},{9,... | collective-permute-start | bytes 1228808 | tf_op jit(solution)/shard_map/ppermute | solution.py:50
  77.4 0.8 copy-start.5
  81.5 33.0 %collective-permute-start.1 = (f32[5,5,2,2,8,128]{5,4,3,2,1,0:T(8,128)}, f32[5,5,2,2,8,128]{5,4,3,2,1,0:T(8,128)S(1)}, u32[]{:S(2)}, u32[]{:S(2)}) collective-permute-start(f32[5,5,2,2,8,128]{5,4,3,2,1,0:T(8,128)} %both_3_1.1), channel_id=1, source_target_pairs={{0,256},{1,257},{2,258},{3,259},{4,260},{5,261},{6,262},{7,263},{8... | collective-permute-start | bytes 1228808 | tf_op jit(solution)/shard_map/ppermute | solution.py:50
  100.0 0.8 copy-start.7
  104.4 0.8 copy-start.8
  108.8 0.8 copy-start.10
  114.5 0.8 copy-start.9

commit v2 on v1

--- a/solution.py
+++ b/solution.py
@@ -16,7 +16,10 @@
 ROWS = 8
 LANES = 128
 AXES = ("gx", "gy", "gz")
-PIECES = ((0, 3), (3, 2))
+PIECES = ((0, 2), (2, 1), (3, 1), (4, 1))
+HOLD = 0
+GROUPS = ((0, 3), (3, 4))
+VMEM_BYTES = 16 * 2**20
 ROUNDER = 1.5 * 2.0**23
 SINE = (4.442867903031852, -7.307443421308049, 3.594788078718595, -0.784374031470659)
 COSINE = (
@@ -44,9 +47,25 @@
 TABLE = lagrange_table()
 
 
-def from_partner(value, stride):
-    mask = 2**stride
-    pairs = [(source, source ^ mask) for source in range(lax.axis_size(AXES))]
+def kind_of(index_x, index_y, index_z, half_x, half_y):
+    return index_x % half_x ^ index_y % half_y ^ index_z
+
+
+def parity(bits):
+    return (bits ^ bits >> 1 ^ bits >> 2) & 1
+
+
+def exchange(value, second):
+    size_x, size_y, size_z = (lax.axis_size(axis) for axis in AXES)
+    pairs = []
+    for device in range(size_x * size_y * size_z):
+        x, y, z = device // (size_y * size_z), device // size_z % size_y, device % size_z
+        kind = parity(kind_of(x, y, z, size_x // 2, size_y // 2))
+        if kind == int(second):
+            x = (x + size_x // 2) % size_x
+        else:
+            y = (y + size_y // 2) % size_y
+        pairs.append((device, (x * size_y + y) * size_z + z))
     return lax.ppermute(value, AXES, pairs)
 
 
@@ -112,6 +131,7 @@
         self.z = (self.along_z + 0.5) / TZ
         self.y = (self.along_y + 0.5) / TY
         self.table = table
+        self.half = half
         self.side_x, self.side_y = sides[0], sides[1]
         self.sign_x = 1.0 - 2.0 * self.side_x.astype(jnp.float32)
         self.sign_y = 1.0 - 2.0 * self.side_y.astype(jnp.float32)
@@ -147,8 +167,8 @@
         cycles = (x[m] + rows) + speed * at.radius(which, m, q, r)
         point = (end(flip_x, m), end(flip_y, q), r_local)
         value = (
-            weights[(*point, pl.ds(0, ROWS, stride=2), slice(None))],
-            weights[(*point, pl.ds(1, ROWS, stride=2), slice(None))],
+            weights[(*point, pl.ds(2 * ROWS * at.half, ROWS, stride=2), slice(None))],
+            weights[(*point, pl.ds(2 * ROWS * at.half + 1, ROWS, stride=2), slice(None))],
         )
         turned.append(backward(value, cycles))
     return merge(turned)
@@ -172,7 +192,8 @@
             + speeds[0] * at.radius(tables[0], p, q, r)
             - speeds[1] * at.radius(tables[1], p, q, r)
         )
-        turned.append(forward((level[p, q, r_local, 0], level[p, q, r_local, 1]), cycles))
+        value = (level[p, q, r_local, at.half, 0], level[p, q, r_local, at.half, 1])
+        turned.append(forward(value, cycles))
     return merge(turned)
 
 
@@ -181,12 +202,11 @@
     ref[(*place, 1)] = values[1]
 
 
-def level_kernel(first, count, table, sides, speeds, own, got, level, send):
-    at = Targets(0, table, sides, speeds)
+def parent(at, first, count, own, got, level):
     x = at.x(False)
     x_own, x_got = first_x(at.sign_x, x), first_x(-at.sign_x, x)
 
-    def one_level(q, carry):
+    def one(q, carry):
         for k in range(count):
             mine = first_merge(
                 at, own, 0, at.sign_x, at.sign_y, (at.side_x, at.side_y), x_own, at.speeds[0], q, first + k, k
@@ -195,26 +215,25 @@
                 at, got, 1, -at.sign_x, at.sign_y, (1 - at.side_x, at.side_y), x_got, at.speeds[0], q, first + k, k
             )
             for p, value in enumerate(flipped(mine, theirs)):
-                put(level, value, p, q, k)
+                put(level, value, p, q, k, at.half)
         return carry
 
-    lax.fori_loop(0, CHEB, one_level, 0)
-    between = between_y(at, at.sign_y, at.fine_y(True))
-
-    def two_level(p, carry):
+    lax.fori_loop(0, CHEB, one, 0)
+
+
+def share_kind_0(at, first, count, far, level, use):
+    between = between_y(at, at.sign_y, at.fine_y(far))
+    speeds = (at.speeds[0], at.speeds[3 if far else 2])
+
+    def one(p, carry):
         for k in range(count):
-            shares = second_merge(
-                at, level, (3, 5), between, (at.speeds[0], at.speeds[3]), p, first + k, k
-            )
-            for q, value in enumerate(shares):
-                put(send, value, p, q, k)
+            use(second_merge(at, level, (3, 5), between, speeds, p, first + k, k), p, k)
         return carry
 
-    lax.fori_loop(0, CHEB, two_level, 0)
-
-
-def both_kernel(first, count, far, table, sides, speeds, own, got, send, level_own, level_got):
-    at = Targets(1, table, sides, speeds)
+    lax.fori_loop(0, CHEB, one, 0)
+
+
+def share_kind_1(at, first, count, far, own, got, level_own, level_got, use):
     x = first_x(at.sign_x, at.x(far))
     speed, speed_two = at.speeds[int(far)], at.speeds[4 if far else 2]
 
@@ -228,7 +247,7 @@
                     at, weights, which, at.sign_x, sign_y, (at.side_x, flip_y), x, speed, q, first + k, k
                 )
                 for p, value in enumerate(merged):
-                    put(level, value, p, q, k)
+                    put(level, value, p, q, k, at.half)
         return carry
 
     lax.fori_loop(0, CHEB, one_level, 0)
@@ -239,102 +258,119 @@
         for k in range(count):
             mine = second_merge(at, level_own, (3, 5), between_own, (speed, speed_two), p, first + k, k)
             theirs = second_merge(at, level_got, (4, 6), between_got, (speed, speed_two), p, first + k, k)
-            for q, value in enumerate(flipped(mine, theirs)):
-                put(send, value, p, q, k)
+            use(flipped(mine, theirs), p, k)
         return carry
 
     lax.fori_loop(0, CHEB, two_level, 0)
 
 
-def last_kernel(half, first, table, sides, speeds, level, got, *rest):
+def piece_kernel(first, count, table, sides, speeds, own, got, send, keep, level, level_got):
+    for half in range(2):
+        at = Targets(half, table, sides, speeds)
+        x, fine = at.x(False), at.fine_y(False)
+        along_y = [fraction((at.sign_y * float(128.0 * z)) * fine) for z in POINTS]
+
+        def to_send(values, p, k, half=half):
+            for q, value in enumerate(values):
+                put(send, value, p, q, k, half)
+
+        def to_keep(values, p, k, at=at, x=x, along_y=along_y):
+            along_x = fraction((at.sign_x * 128.0 * at.point(p)) * x)
+            along_xz = fraction(along_x + float(64.0 * POINTS[first + k]) * at.z)
+            for q, value in enumerate(values):
+                cycles = (along_xz + along_y[q]) + at.speeds[2] * at.radius(7, p, q, first + k)
+                cosine, sine = turn(cycles)
+                place = (p, q, k, at.half)
+                keep[(*place, 0)] = value[0] * cosine - value[1] * sine
+                keep[(*place, 1)] = value[0] * sine + value[1] * cosine
+                keep[(*place, 2)] = cosine
+                keep[(*place, 3)] = sine
+
+        @pl.when(sides[2] == 0)
+        def _(at=at, to_send=to_send, to_keep=to_keep):
+            parent(at, first, count, own, got, level)
+            share_kind_0(at, first, count, True, level, to_send)
+            share_kind_0(at, first, count, False, level, to_keep)
+
+        @pl.when(sides[2] == 1)
+        def _(at=at, to_send=to_send, to_keep=to_keep):
+            share_kind_1(at, first, count, True, own, got, level, level_got, to_send)
+            share_kind_1(at, first, count, False, own, got, level, level_got, to_keep)
+
+
+def last_kernel(pieces, sides, *rest):
     out = rest[-1]
-    at = Targets(half, table, sides, speeds)
-    r = first + pl.program_id(0)
-    x, fine = at.x(False), at.fine_y(False)
-    along_y = [fraction((at.sign_y * float(128.0 * z)) * fine) for z in POINTS]
-    along_z = fraction(at.point(r) * 64.0 * at.z)
-    along_yz = [value + along_z for value in along_y]
-    between = between_y(at, at.sign_y, fine)
-
-    def one_p(p, carry):
-        along_x = fraction((at.sign_x * 128.0 * at.point(p)) * x)
-        if half == 0:
-            mine = second_merge(
-                at, level, (3, 5), between, (at.speeds[0], at.speeds[2]), p, r, 0
-            )
+    side_x, side_y, kind = sides[0], sides[1], sides[2]
+
+    def one(p, carry):
         for q in range(CHEB):
-            if half == 0:
-                value = mine[q]
-                other = (got[p, CHEB - 1 - q, 0, 0], got[p, CHEB - 1 - q, 0, 1])
-            else:
-                value = (level[p, q, 0, 0], level[p, q, 0, 1])
-                other = (got[CHEB - 1 - p, q, 0, 0], got[CHEB - 1 - p, q, 0, 1])
-            cycles = (along_x + along_yz[q]) + at.speeds[2] * at.radius(7, p, q, r)
-            value = forward((value[0] + other[0], value[1] + other[1]), cycles)
-            point = (end(at.side_x, p), end(at.side_y, q), 0)
-            out[(*point, pl.ds(0, ROWS, stride=2), slice(None))] = value[0]
-            out[(*point, pl.ds(1, ROWS, stride=2), slice(None))] = value[1]
+            point = (end(side_x, p), end(side_y, q))
+            other = (end(kind, p), end(1 - kind, q))
+            for place, (ref, k) in enumerate(pieces):
+                keep, got = rest[2 * ref], rest[2 * ref + 1]
+                for half in range(2):
+                    re, im = got[(*other, k, half, 0)], got[(*other, k, half, 1)]
+                    cosine, sine = keep[p, q, k, half, 2], keep[p, q, k, half, 3]
+                    real = keep[p, q, k, half, 0] + (re * cosine - im * sine)
+                    imaginary = keep[p, q, k, half, 1] + (re * sine + im * cosine)
+                    row = 2 * ROWS * half
+                    out[(*point, place, pl.ds(row, ROWS, stride=2), slice(None))] = real
+                    out[(*point, place, pl.ds(row + 1, ROWS, stride=2), slice(None))] = imaginary
         return carry
 
-    lax.fori_loop(0, CHEB, one_p, 0)
+    lax.fori_loop(0, CHEB, one, 0)
 
 
 SMEM = pl.BlockSpec(memory_space=pltpu.SMEM)
 VMEM = pl.BlockSpec(memory_space=pltpu.VMEM)
-
-
-def complex_shape(count):
-    return (CHEB, CHEB, count, 2, ROWS, LANES)
+PARAMS = pltpu.CompilerParams(vmem_limit_bytes=VMEM_BYTES)
+
+
+def pieces_of(count, parts):
+    return (CHEB, CHEB, count, 2, parts, ROWS, LANES)
 
 
 def cost(sets):
     return pl.CostEstimate(flops=sets * ROWS * LANES * 60, bytes_accessed=sets * 20000, transcendentals=0)
 
 
-def run_level(first, count, facts, own, got):
-    shape = jax.ShapeDtypeStruct(complex_shape(count), jnp.float32)
+def run_piece(first, count, facts, own, got):
     return pl.pallas_call(
-        functools.partial(level_kernel, first, count),
+        functools.partial(piece_kernel, first, count),
         in_specs=[SMEM, SMEM, VMEM, VMEM, VMEM],
         out_specs=[VMEM, VMEM],
-        out_shape=[shape, shape],
-        cost_estimate=cost(75 * count),
-        name=f"level_{first}",
+        out_shape=[jax.ShapeDtypeStruct(pieces_of(count, parts), jnp.float32) for parts in (2, 4)],
+        scratch_shapes=[pltpu.VMEM(pieces_of(count, 2), jnp.float32)] * 2,
+        compiler_params=PARAMS,
+        cost_estimate=cost(450 * count),
+        name=f"piece_{first}",
     )(*facts, own, got)
 
 
-def run_both(first, count, far, facts, own, got):
-    return pl.pallas_call(
-        functools.partial(both_kernel, first, count, far),
-        in_specs=[SMEM, SMEM, VMEM, VMEM, VMEM],
-        out_specs=VMEM,
-        out_shape=jax.ShapeDtypeStruct(complex_shape(count), jnp.float32),
-        scratch_shapes=[pltpu.VMEM(complex_shape(count), jnp.float32)] * 2,
-        cost_estimate=cost(100 * count),
-        name=f"both_{first}_{int(far)}",
-    )(*facts, own, got)
-
-
-def run_last(half, first, count, facts, level, got, out):
-    block = (CHEB, CHEB, 1, 2, ROWS, LANES)
-    in_specs = [SMEM, SMEM, VMEM] + [pl.BlockSpec(block, lambda i: (0, 0, i, 0, 0, 0))] * 2
-    operands = [*facts, level, got]
+def run_last(group, facts, kept, arrived, out):
+    pieces = [(ref, k) for ref, (_, count) in enumerate(PIECES[slice(*group)]) for k in range(count)]
+    first, count = PIECES[group[0]][0], len(pieces)
+    operands = [facts[1]]
+    for piece in range(*group):
+        operands += [kept[piece], arrived[piece]]
+    in_specs = [SMEM] + [VMEM] * (len(operands) - 1)
     aliases = {}
     if out is not None:
+        aliases = {len(operands): 0}
         in_specs.append(pl.BlockSpec(memory_space=pl.ANY))
         operands.append(out)
-        aliases = {5: 0}
     return pl.pallas_call(
-        functools.partial(last_kernel, half, first),
-        grid=(count,),
+        functools.partial(last_kernel, pieces),
+        grid=(1,),
         in_specs=in_specs,
         out_specs=pl.BlockSpec(
-            (CHEB, CHEB, 1, 2 * ROWS, LANES), lambda i: (0, 0, first + i, half, 0)
+            (CHEB, CHEB, count, 4 * ROWS, LANES), lambda i: (0, 0, first // count, 0, 0)
         ),
         out_shape=jax.ShapeDtypeStruct((CHEB, CHEB, CHEB, 4 * ROWS, LANES), jnp.float32),
         input_output_aliases=aliases,
-        cost_estimate=cost(50 * count),
-        name=f"last_{half}_{first}",
+        compiler_params=PARAMS,
+        cost_estimate=cost(25 * count),
+        name=f"last_{first}",
     )(*operands)
 
 
@@ -388,7 +424,8 @@
     last = np.zeros((8, LANES), np.float32)
     last[0, :CHEB] = POINTS
     table = jnp.concatenate([numerator / radius, last], 0)
-    sides = jnp.stack([side_x, side_y]).astype(jnp.int32)
+    kind = parity(kind_of(index_x, index_y, index_z, half_x, half_y))
+    sides = jnp.stack([side_x, side_y, kind]).astype(jnp.int32)
 
     first = speed_first.reshape(TX, 2, TY * TZ)
     first_own = jnp.where(side_x == 0, first[:, 0], first[:, 1])
@@ -407,31 +444,25 @@
 
 
 def shards(source_coefs, speed_first, speed_second):
-    bit_first = (lax.axis_size("gx") * lax.axis_size("gy") * lax.axis_size("gz")).bit_length() - 2
-    bit_second = (lax.axis_size("gy") * lax.axis_size("gz")).bit_length() - 2
     weights = source_coefs.reshape(2, CHEB, CHEB, CHEB, 2 * ROWS, LANES)
     weights = weights.transpose(1, 2, 3, 4, 0, 5).reshape(CHEB, CHEB, CHEB, 4 * ROWS, LANES)
-    raw = [
-        [weights[:, :, first : first + count, 16 * half : 16 * (half + 1)] for first, count in PIECES]
-        for half in range(2)
-    ]
-    got = [[], []]
-    for k in range(len(PIECES)):
-        got[0].append(from_partner(raw[0][k], bit_first))
-        got[1].append(from_partner(raw[1][k], bit_second))
+    raw = [weights[:, :, first : first + count] for first, count in PIECES]
+    got = [exchange(piece, False) for piece in raw]
     facts = device_facts(speed_first, speed_second)
-    levels, shares, arrived, arrived_two = [], [], [], []
+    sent, kept = [], []
     for k, (first, count) in enumerate(PIECES):
-        level, send = run_level(first, count, facts, raw[0][k], got[0][k])
-        levels.append(level)
-        arrived.append(from_partner(send, bit_second))
-        send = run_both(first, count, True, facts, raw[1][k], got[1][k])
-        arrived_two.append(from_partner(send, bit_first))
-        shares.append(run_both(first, count, False, facts, raw[1][k], got[1][k]))
+        send, keep = run_piece(first, count, facts, raw[k], got[k])
+        sent.append(send)
+        kept.append(keep)
+    arrived = []
+    for k, send in enumerate(sent):
+        later = min(k + HOLD, len(sent) - 1)
+        if later > k:
+            send, sent[later] = lax.optimization_barrier((send, sent[later]))
+        arrived.append(exchange(send, True))
     out = None
-    for k, (first, count) in enumerate(PIECES):
-        out = run_last(0, first, count, facts, levels[k], arrived[k], out)
-        out = run_last(1, first, count, facts, shares[k], arrived_two[k], out)
+    for group in GROUPS:
+        out = run_last(group, facts, kept, arrived, out)
     out = out.reshape(CHEB, CHEB, CHEB, 2 * ROWS, 2, LANES).transpose(4, 0, 1, 2, 3, 5)
     return out.reshape(source_coefs.shape)
 

time: 118 us -> 108 us (0.915)
  the two profiles are of different devices: /device:TPU:21 before, /device:TPU:36 now
where the time goes in v2:
time: 108 us; the launch traced here: 107 us
  starting transfers between devices  59.7 us (55%)
  Pallas kernels  23.1 us (21%)
  waiting for transfers between devices  14.5 us (13%)
  local copies, waits for them, and re-layouts  5.07 us (5%)
  other arithmetic  4.68 us (4%)
    ppermute x8, starting transfers between devices, exchange(): return lax.ppermute(value, AXES, pairs)  59.7 us
    pallas_call x4, Pallas kernels, run_piece(): pl.pallas_call(functools.partial(piece_kernel, first, count), in_specs=[S...  19.6 us
    ppermute x8, waiting for transfers between devices, exchange(): return lax.ppermute(value, AXES, pairs)  14.5 us
    pallas_call x2, Pallas kernels, run_last(): pl.pallas_call(functools.partial(last_kernel, pieces), grid=(1,), in_spec...  3.5 us
    slice x2, local copies, waits for them, and re-layouts, shards(): raw = [weights[:, :, first:first + count] for first, count in PIECES]  2.58 us
  transfers between devices with their start and end apart: 8, of which 3 were waited for; matrix products, arithmetic and copies ran while one was open for 8% of the time, Pallas kernels for 20%

profile of v2, /device:TPU:36, one launch (start us, length us, event | category | flops | bytes accessed | tf_op | source)
XLA Modules:
  0.0 107.3 jit_solution(16167722036424248636)
XLA Ops:
  0.0 1.2 %slice.63.own = f32[5,5,2,32,128]{4,3,2,1,0:T(8,128)S(1)} slice(f32[5,5,5,32,128]{4,3,2,1,0:T(8,128)} %bitcast.55), slice={[0:5], [0:5], [0:2], [0:32], [0:128]} | slice | bytes 1638400 | tf_op jit(solution)/shard_map/slice | solution.py:449
  1.2 0.0 copy-start.3
  1.2 0.0 copy-start.1
  1.2 0.0 copy-start.2
  1.3 0.0 copy-start
  1.3 2.1 %collective-permute-start.2 = (f32[5,5,2,32,128]{4,3,2,1,0:T(8,128)S(1)}, f32[5,5,2,32,128]{4,3,2,1,0:T(8,128)S(1)}, u32[]{:S(2)}, u32[]{:S(2)}) collective-permute-start(f32[5,5,2,32,128]{4,3,2,1,0:T(8,128)S(1)} %slice.63.own), channel_id=1, source_target_pairs={{0,256},{1,33},{2,34},{3,259},{4,36},{5,261},{6,262},{7,39},{8,40}... | collective-permute-start | bytes 2457608 | tf_op jit(solution)/shard_map/ppermute | solution.py:69
  3.4 1.4 %fusion.12 = (f32[5,5,1,32,128]{4,3,2,1,0:T(8,128)S(1)}, f32[5,5,1,32,128]{4,3,2,1,0:T(8,128)S(1)}, f32[5,5,1,32,128]{4,3,2,1,0:T(8,128)S(1)}) fusion(f32[5,5,5,32,128]{4,3,2,1,0:T(8,128)} %bitcast.56), kind=kLoop, calls=%fused_computation.36 | loop fusion | bytes 2457600 | tf_op jit(solution)/shard_map/slice | solution.py:449
  4.8 7.7 %collective-permute-start.6 = (f32[5,5,1,32,128]{4,3,2,1,0:T(8,128)S(1)}, f32[5,5,1,32,128]{4,3,2,1,0:T(8,128)}, u32[]{:S(2)}, u32[]{:S(2)}) collective-permute-start(f32[5,5,1,32,128]{4,3,2,1,0:T(8,128)S(1)} %get-tuple-element.23.own), channel_id=1, source_target_pairs={{0,256},{1,33},{2,34},{3,259},{4,36},{5,261},{6,262},{7,39},{8,40}... | collective-permute-start | bytes 1228808 | tf_op jit(solution)/shard_map/ppermute | solution.py:69
  12.5 2.0 %collective-permute-start.4 = (f32[5,5,1,32,128]{4,3,2,1,0:T(8,128)S(1)}, f32[5,5,1,32,128]{4,3,2,1,0:T(8,128)}, u32[]{:S(2)}, u32[]{:S(2)}) collective-permute-start(f32[5,5,1,32,128]{4,3,2,1,0:T(8,128)S(1)} %get-tuple-element.24.own), channel_id=1, source_target_pairs={{0,256},{1,33},{2,34},{3,259},{4,36},{5,261},{6,262},{7,39},{8,40}... | collective-permute-start | bytes 1228808 | tf_op jit(solution)/shard_map/ppermute | solution.py:69
  14.6 7.7 %collective-permute-start = (f32[5,5,1,32,128]{4,3,2,1,0:T(8,128)S(1)}, f32[5,5,1,32,128]{4,3,2,1,0:T(8,128)S(1)}, u32[]{:S(2)}, u32[]{:S(2)}) collective-permute-start(f32[5,5,1,32,128]{4,3,2,1,0:T(8,128)S(1)} %get-tuple-element.25.own), channel_id=1, source_target_pairs={{0,256},{1,33},{2,34},{3,259},{4,36},{5,261},{6,262},{7,39},{8,40}... | collective-permute-start | bytes 1228808 | tf_op jit(solution)/shard_map/ppermute | solution.py:69
  22.4 1.0 copy.19
  23.4 0.7 fusion.1
  24.1 0.7 fusion
  24.8 1.0 reshape.190
  25.9 0.7 fusion.10
  26.6 0.1 stack.81
  26.7 0.0 copy-done.3
  26.7 0.7 fusion.5
  27.3 0.0 copy-done.1
  27.3 0.0 copy-done.2
  27.4 0.1 add_divide_fusion
  27.5 1.7 %fusion.3 = (f32[8,16,16]{2,1,0:T(8,128)S(1)}, f32[8,16,16]{2,1,0:T(8,128)S(1)}, f32[8,16,16]{2,1,0:T(8,128)S(1)}) fusion(pred[]{:T(512)S(6)} %eq.17, f32[8,16,2,16]{3,2,1,0:T(2,128)} %fusion.1, f32[8,16,2,16]{3,2,1,0:T(2,128)} %fusion), kind=kLoop, calls=%fused_computation.8 | loop fusion | flops 6144 | bytes 57345 | tf_op jit(solution)/shard_map/jit(_where)/select_n | solution.py:440
  29.2 0.1 select_n.134
  29.3 0.1 select_n.132
  29.4 0.1 select_n.138
  29.5 0.0 copy-done
  29.5 0.1 pad_add_fusion.sides
  29.6 0.0 collective-permute-done.2.got
  29.6 6.7 %piece_0.1 = (f32[5,5,2,2,2,8,128]{6,5,4,3,2,1,0:T(8,128)S(1)}, f32[5,5,2,2,4,8,128]{6,5,4,3,2,1,0:T(8,128)S(1)}) custom-call(f32[16,128]{1,0:T(8,128)S(1)} %pad_maximum_fusion.table, s32[3]{0:T(128)S(1)} %pad_add_fusion.sides, f32[5,16,128]{2,1,0:T(8,128)S(1)} %constant_dynamic-update-slice_fusion.speeds, f32[5,5,2,32,128]{4,3,2,1,0:T(8,128)S(1)} %slice.63.own, ...), custom_call_target="tpu_custom_call" | custom-call | flops 55296000 | bytes 18000000 | tf_op jit(solution)/shard_map/piece_0/pallas_call | solution.py:338
  36.3 10.9 %collective-permute-start.3 = (f32[5,5,2,2,2,8,128]{6,5,4,3,2,1,0:T(8,128)S(1)}, f32[5,5,2,2,2,8,128]{6,5,4,3,2,1,0:T(8,128)S(1)}, u32[]{:S(2)}, u32[]{:S(2)}) collective-permute-start(f32[5,5,2,2,2,8,128]{6,5,4,3,2,1,0:T(8,128)S(1)} %get-tuple-element.16), channel_id=1, source_target_pairs={{0,32},{1,257},{2,258},{3,35},{4,260},{5,37},{6,38},{7,263},{8,264... | collective-permute-start | bytes 2457608 | tf_op jit(solution)/shard_map/ppermute | solution.py:69
  47.2 0.0 collective-permute-done.6.got
  47.3 4.4 %piece_3.1 = (f32[5,5,1,2,2,8,128]{6,5,4,3,2,1,0:T(8,128)S(1)}, f32[5,5,1,2,4,8,128]{6,5,4,3,2,1,0:T(8,128)S(1)}) custom-call(f32[16,128]{1,0:T(8,128)S(1)} %pad_maximum_fusion.table, s32[3]{0:T(128)S(1)} %pad_add_fusion.sides, f32[5,16,128]{2,1,0:T(8,128)S(1)} %constant_dynamic-update-slice_fusion.speeds, f32[5,5,1,32,128]{4,3,2,1,0:T(8,128)S(1)} %get-tuple-element.23.own, ...), custom_call_target="tpu_custom_call" | custom-call | flops 27648000 | bytes 9000000 | tf_op jit(solution)/shard_map/piece_3/pallas_call | solution.py:338
  51.7 3.4 %collective-permute-start.7 = (f32[5,5,1,2,2,8,128]{6,5,4,3,2,1,0:T(8,128)S(1)}, f32[5,5,1,2,2,8,128]{6,5,4,3,2,1,0:T(8,128)S(1)}, u32[]{:S(2)}, u32[]{:S(2)}) collective-permute-start(f32[5,5,1,2,2,8,128]{6,5,4,3,2,1,0:T(8,128)S(1)} %get-tuple-element.20), channel_id=1, source_target_pairs={{0,32},{1,257},{2,258},{3,35},{4,260},{5,37},{6,38},{7,263},{8,264... | collective-permute-start | bytes 1228808 | tf_op jit(solution)/shard_map/ppermute | solution.py:69
  55.1 5.1 %collective-permute-done.4.got = f32[5,5,1,32,128]{4,3,2,1,0:T(8,128)} collective-permute-done((f32[5,5,1,32,128]{4,3,2,1,0:T(8,128)S(1)}, f32[5,5,1,32,128]{4,3,2,1,0:T(8,128)}, u32[]{:S(2)}, u32[]{:S(2)}) %collective-permute-start.4) | collective-permute-done | bytes 409632 | tf_op jit(solution)/shard_map/ppermute | solution.py:69
  60.2 4.4 %piece_2.1 = (f32[5,5,1,2,2,8,128]{6,5,4,3,2,1,0:T(8,128)S(1)}, f32[5,5,1,2,4,8,128]{6,5,4,3,2,1,0:T(8,128)S(1)}) custom-call(f32[16,128]{1,0:T(8,128)S(1)} %pad_maximum_fusion.table, s32[3]{0:T(128)S(1)} %pad_add_fusion.sides, f32[5,16,128]{2,1,0:T(8,128)S(1)} %constant_dynamic-update-slice_fusion.speeds, f32[5,5,1,32,128]{4,3,2,1,0:T(8,128)S(1)} %get-tuple-element.24.own, ...), custom_call_target="tpu_custom_call" | custom-call | flops 27648000 | bytes 9000000 | tf_op jit(solution)/shard_map/piece_2/pallas_call | solution.py:338
  64.6 12.0 %collective-permute-start.5 = (f32[5,5,1,2,2,8,128]{6,5,4,3,2,1,0:T(8,128)S(1)}, f32[5,5,1,2,2,8,128]{6,5,4,3,2,1,0:T(8,128)S(1)}, u32[]{:S(2)}, u32[]{:S(2)}) collective-permute-start(f32[5,5,1,2,2,8,128]{6,5,4,3,2,1,0:T(8,128)S(1)} %get-tuple-element.18), channel_id=1, source_target_pairs={{0,32},{1,257},{2,258},{3,35},{4,260},{5,37},{6,38},{7,263},{8,264... | collective-permute-start | bytes 1228808 | tf_op jit(solution)/shard_map/ppermute | solution.py:69
  76.7 5.3 %collective-permute-done.got = f32[5,5,1,32,128]{4,3,2,1,0:T(8,128)S(1)} collective-permute-done((f32[5,5,1,32,128]{4,3,2,1,0:T(8,128)S(1)}, f32[5,5,1,32,128]{4,3,2,1,0:T(8,128)S(1)}, u32[]{:S(2)}, u32[]{:S(2)}) %collective-permute-start) | collective-permute-done | bytes 409632 | tf_op jit(solution)/shard_map/ppermute | solution.py:69
  82.0 4.1 %piece_4.1 = (f32[5,5,1,2,2,8,128]{6,5,4,3,2,1,0:T(8,128)S(1)}, f32[5,5,1,2,4,8,128]{6,5,4,3,2,1,0:T(8,128)S(1)}) custom-call(f32[16,128]{1,0:T(8,128)S(1)} %pad_maximum_fusion.table, s32[3]{0:T(128)S(1)} %pad_add_fusion.sides, f32[5,16,128]{2,1,0:T(8,128)S(1)} %constant_dynamic-update-slice_fusion.speeds, f32[5,5,1,32,128]{4,3,2,1,0:T(8,128)S(1)} %get-tuple-element.25.own, ...), custom_call_target="tpu_custom_call" | custom-call | flops 27648000 | bytes 9000000 | tf_op jit(solution)/shard_map/piece_4/pallas_call | solution.py:338
  86.0 13.7 %collective-permute-start.1 = (f32[5,5,1,2,2,8,128]{6,5,4,3,2,1,0:T(8,128)S(1)}, f32[5,5,1,2,2,8,128]{6,5,4,3,2,1,0:T(8,128)S(1)}, u32[]{:S(2)}, u32[]{:S(2)}) collective-permute-start(f32[5,5,1,2,2,8,128]{6,5,4,3,2,1,0:T(8,128)S(1)} %get-tuple-element.14), channel_id=1, source_target_pairs={{0,32},{1,257},{2,258},{3,35},{4,260},{5,37},{6,38},{7,263},{8,264... | collective-permute-start | bytes 1228808 | tf_op jit(solution)/shard_map/ppermute | solution.py:69
  99.7 0.0 collective-permute-done.7.rest_5_
  99.8 0.0 collective-permute-done.5.rest_3_
  99.8 0.0 collective-permute-done.3.rest_1_
  99.8 2.1 %last_0.1.rest_2_ = f32[5,5,5,32,128]{4,3,2,1,0:T(8,128)} custom-call(s32[3]{0:T(128)S(1)} %pad_add_fusion.sides, f32[5,5,2,2,4,8,128]{6,5,4,3,2,1,0:T(8,128)S(1)} %get-tuple-element.15.rest_0_, f32[5,5,2,2,2,8,128]{6,5,4,3,2,1,0:T(8,128)S(1)} %collective-permute-done.3.rest_1_, f32[5,5,1,2,4,8,128]{6,5,4,3,2,1,0:T(8,128)S(1)} %get-tuple-element.17.rest_2_, ...), custom_call_target="tpu_custom_call" | custom-call | flops 6144000 | bytes 2000000 | tf_op jit(solution)/shard_map/last_0/pallas_call | solution.py:362
  101.9 4.1 %collective-permute-done.1.rest_1_ = f32[5,5,1,2,2,8,128]{6,5,4,3,2,1,0:T(8,128)S(1)} collective-permute-done((f32[5,5,1,2,2,8,128]{6,5,4,3,2,1,0:T(8,128)S(1)}, f32[5,5,1,2,2,8,128]{6,5,4,3,2,1,0:T(8,128)S(1)}, u32[]{:S(2)}, u32[]{:S(2)}) %collective-permute-start.1) | collective-permute-done | bytes 409632 | tf_op jit(solution)/shard_map/ppermute | solution.py:69
  105.9 1.4 %last_4.1 = f32[5,5,5,32,128]{4,3,2,1,0:T(8,128)} custom-call(s32[3]{0:T(128)S(1)} %pad_add_fusion.sides, f32[5,5,1,2,4,8,128]{6,5,4,3,2,1,0:T(8,128)S(1)} %get-tuple-element.13.rest_0_, f32[5,5,1,2,2,8,128]{6,5,4,3,2,1,0:T(8,128)S(1)} %collective-permute-done.1.rest_1_, f32[5,5,5,32,128]{4,3,2,1,0:T(8,128)} %last_0.1.rest_2_), custom_call_target="tpu_custom_call", output_to_operand_aliasing={{}: (3, {})} | custom-call | flops 1536000 | bytes 500000 | tf_op jit(solution)/shard_map/last_4/pallas_call | solution.py:362
  (14 shorter events, 0.1 us)
Async XLA Ops:
  1.2 25.4 %copy-start.3 = (f32[128]{0:T(128)S(1)}, f32[128]{0:T(128)}, u32[]{:S(2)}) copy-start(f32[128]{0:T(128)} %constant.82.clone) | copy-start | bytes 1540
  1.2 26.1 %copy-start.1 = (f32[128]{0:T(128)S(1)}, f32[128]{0:T(128)}, u32[]{:S(2)}) copy-start(f32[128]{0:T(128)} %constant.84.clone) | copy-start | bytes 1540
  1.2 26.1 %copy-start.2 = (f32[128]{0:T(128)S(1)}, f32[128]{0:T(128)}, u32[]{:S(2)}) copy-start(f32[128]{0:T(128)} %constant.83.clone) | copy-start | bytes 1540
  1.3 28.2 %copy-start = (f32[8,128]{1,0:T(8,128)S(1)}, f32[8,128]{1,0:T(8,128)}, u32[]{:S(2)}) copy-start(f32[8,128]{1,0:T(8,128)} %constant.86.clone) | copy-start | bytes 12292
  1.3 28.4 %collective-permute-start.2 = (f32[5,5,2,32,128]{4,3,2,1,0:T(8,128)S(1)}, f32[5,5,2,32,128]{4,3,2,1,0:T(8,128)S(1)}, u32[]{:S(2)}, u32[]{:S(2)}) collective-permute-start(f32[5,5,2,32,128]{4,3,2,1,0:T(8,128)S(1)} %slice.63.own), channel_id=1, source_target_pairs={{0,256},{1,33},{2,34},{3,259},{4,36},{5,261},{6,262},{7,39},{8,40}... | collective-permute-start | bytes 2457608 | tf_op jit(solution)/shard_map/ppermute | solution.py:69
  4.8 42.4 %collective-permute-start.6 = (f32[5,5,1,32,128]{4,3,2,1,0:T(8,128)S(1)}, f32[5,5,1,32,128]{4,3,2,1,0:T(8,128)}, u32[]{:S(2)}, u32[]{:S(2)}) collective-permute-start(f32[5,5,1,32,128]{4,3,2,1,0:T(8,128)S(1)} %get-tuple-element.23.own), channel_id=1, source_target_pairs={{0,256},{1,33},{2,34},{3,259},{4,36},{5,261},{6,262},{7,39},{8,40}... | collective-permute-start | bytes 1228808 | tf_op jit(solution)/shard_map/ppermute | solution.py:69
  12.5 47.7 %collective-permute-start.4 = (f32[5,5,1,32,128]{4,3,2,1,0:T(8,128)S(1)}, f32[5,5,1,32,128]{4,3,2,1,0:T(8,128)}, u32[]{:S(2)}, u32[]{:S(2)}) collective-permute-start(f32[5,5,1,32,128]{4,3,2,1,0:T(8,128)S(1)} %get-tuple-element.24.own), channel_id=1, source_target_pairs={{0,256},{1,33},{2,34},{3,259},{4,36},{5,261},{6,262},{7,39},{8,40}... | collective-permute-start | bytes 1228808 | tf_op jit(solution)/shard_map/ppermute | solution.py:69
  14.6 67.4 %collective-permute-start = (f32[5,5,1,32,128]{4,3,2,1,0:T(8,128)S(1)}, f32[5,5,1,32,128]{4,3,2,1,0:T(8,128)S(1)}, u32[]{:S(2)}, u32[]{:S(2)}) collective-permute-start(f32[5,5,1,32,128]{4,3,2,1,0:T(8,128)S(1)} %get-tuple-element.25.own), channel_id=1, source_target_pairs={{0,256},{1,33},{2,34},{3,259},{4,36},{5,261},{6,262},{7,39},{8,40}... | collective-permute-start | bytes 1228808 | tf_op jit(solution)/shard_map/ppermute | solution.py:69
  36.3 63.4 %collective-permute-start.3 = (f32[5,5,2,2,2,8,128]{6,5,4,3,2,1,0:T(8,128)S(1)}, f32[5,5,2,2,2,8,128]{6,5,4,3,2,1,0:T(8,128)S(1)}, u32[]{:S(2)}, u32[]{:S(2)}) collective-permute-start(f32[5,5,2,2,2,8,128]{6,5,4,3,2,1,0:T(8,128)S(1)} %get-tuple-element.16), channel_id=1, source_target_pairs={{0,32},{1,257},{2,258},{3,35},{4,260},{5,37},{6,38},{7,263},{8,264... | collective-permute-start | bytes 2457608 | tf_op jit(solution)/shard_map/ppermute | solution.py:69
  51.7 48.1 %collective-permute-start.7 = (f32[5,5,1,2,2,8,128]{6,5,4,3,2,1,0:T(8,128)S(1)}, f32[5,5,1,2,2,8,128]{6,5,4,3,2,1,0:T(8,128)S(1)}, u32[]{:S(2)}, u32[]{:S(2)}) collective-permute-start(f32[5,5,1,2,2,8,128]{6,5,4,3,2,1,0:T(8,128)S(1)} %get-tuple-element.20), channel_id=1, source_target_pairs={{0,32},{1,257},{2,258},{3,35},{4,260},{5,37},{6,38},{7,263},{8,264... | collective-permute-start | bytes 1228808 | tf_op jit(solution)/shard_map/ppermute | solution.py:69
  64.6 35.1 %collective-permute-start.5 = (f32[5,5,1,2,2,8,128]{6,5,4,3,2,1,0:T(8,128)S(1)}, f32[5,5,1,2,2,8,128]{6,5,4,3,2,1,0:T(8,128)S(1)}, u32[]{:S(2)}, u32[]{:S(2)}) collective-permute-start(f32[5,5,1,2,2,8,128]{6,5,4,3,2,1,0:T(8,128)S(1)} %get-tuple-element.18), channel_id=1, source_target_pairs={{0,32},{1,257},{2,258},{3,35},{4,260},{5,37},{6,38},{7,263},{8,264... | collective-permute-start | bytes 1228808 | tf_op jit(solution)/shard_map/ppermute | solution.py:69
  86.0 19.9 %collective-permute-start.1 = (f32[5,5,1,2,2,8,128]{6,5,4,3,2,1,0:T(8,128)S(1)}, f32[5,5,1,2,2,8,128]{6,5,4,3,2,1,0:T(8,128)S(1)}, u32[]{:S(2)}, u32[]{:S(2)}) collective-permute-start(f32[5,5,1,2,2,8,128]{6,5,4,3,2,1,0:T(8,128)S(1)} %get-tuple-element.14), channel_id=1, source_target_pairs={{0,32},{1,257},{2,258},{3,35},{4,260},{5,37},{6,38},{7,263},{8,264... | collective-permute-start | bytes 1228808 | tf_op jit(solution)/shard_map/ppermute | solution.py:69

commit v3 on v2

--- a/solution.py
+++ b/solution.py
@@ -298,9 +298,12 @@
             share_kind_1(at, first, count, False, own, got, level, level_got, to_keep)
 
 
-def last_kernel(pieces, sides, *rest):
+def last_kernel(pieces, *rest):
     out = rest[-1]
-    side_x, side_y, kind = sides[0], sides[1], sides[2]
+    half_x, half_y = lax.axis_size("gx") // 2, lax.axis_size("gy") // 2
+    index_x, index_y, index_z = (lax.axis_index(axis) for axis in AXES)
+    side_x, side_y = lax.div(index_x, half_x), lax.div(index_y, half_y)
+    kind = parity(kind_of(index_x, index_y, index_z, half_x, half_y))
 
     def one(p, carry):
         for q in range(CHEB):
@@ -347,13 +350,13 @@
     )(*facts, own, got)
 
 
-def run_last(group, facts, kept, arrived, out):
+def run_last(group, kept, arrived, out):
     pieces = [(ref, k) for ref, (_, count) in enumerate(PIECES[slice(*group)]) for k in range(count)]
     first, count = PIECES[group[0]][0], len(pieces)
-    operands = [facts[1]]
+    operands = []
     for piece in range(*group):
         operands += [kept[piece], arrived[piece]]
-    in_specs = [SMEM] + [VMEM] * (len(operands) - 1)
+    in_specs = [VMEM] * len(operands)
     aliases = {}
     if out is not None:
         aliases = {len(operands): 0}
@@ -462,7 +465,7 @@
         arrived.append(exchange(send, True))
     out = None
     for group in GROUPS:
-        out = run_last(group, facts, kept, arrived, out)
+        out = run_last(group, kept, arrived, out)
     out = out.reshape(CHEB, CHEB, CHEB, 2 * ROWS, 2, LANES).transpose(4, 0, 1, 2, 3, 5)
     return out.reshape(source_coefs.shape)
 

time: 108 us -> 107 us (level)
  Pallas kernels: 23.1 us -> 22 us
    pallas_call x2, Pallas kernels: 3.5 us -> 2.4 us  [run_last(): pl.pallas_call(functools.partial(last_kernel, pieces), grid=(1,), in_spec...]
where the time goes in v3:
time: 107 us
  starting transfers between devices  59.7 us (56%)
  Pallas kernels  22 us (21%)
  waiting for transfers between devices  15 us (14%)
  local copies, waits for them, and re-layouts  5.07 us (5%)
  other arithmetic  4.68 us (4%)
    ppermute x8, starting transfers between devices, exchange(): return lax.ppermute(value, AXES, pairs)  59.7 us
    pallas_call x4, Pallas kernels, run_piece(): pl.pallas_call(functools.partial(piece_kernel, first, count), in_specs=[S...  19.6 us
    ppermute x8, waiting for transfers between devices, exchange(): return lax.ppermute(value, AXES, pairs)  15 us
    slice x2, local copies, waits for them, and re-layouts, shards(): raw = [weights[:, :, first:first + count] for first, count in PIECES]  2.58 us
    pallas_call x2, Pallas kernels, run_last(): pl.pallas_call(functools.partial(last_kernel, pieces), grid=(1,), in_spec...  2.4 us
  transfers between devices with their start and end apart: 8, of which 3 were waited for; matrix products, arithmetic and copies ran while one was open for 8% of the time, Pallas kernels for 20%

profile of v3, /device:TPU:36, one launch (start us, length us, event | category | flops | bytes accessed | tf_op | source)
XLA Modules:
  0.0 106.8 jit_solution(8489450873658954979)
XLA Ops:
  0.0 1.2 %slice.63.own = f32[5,5,2,32,128]{4,3,2,1,0:T(8,128)S(1)} slice(f32[5,5,5,32,128]{4,3,2,1,0:T(8,128)} %bitcast.55), slice={[0:5], [0:5], [0:2], [0:32], [0:128]} | slice | bytes 1638400 | tf_op jit(solution)/shard_map/slice | solution.py:452
  1.2 0.0 copy-start.3
  1.2 0.0 copy-start.1
  1.2 0.0 copy-start.2
  1.3 0.0 copy-start
  1.3 2.1 %collective-permute-start.2 = (f32[5,5,2,32,128]{4,3,2,1,0:T(8,128)S(1)}, f32[5,5,2,32,128]{4,3,2,1,0:T(8,128)S(1)}, u32[]{:S(2)}, u32[]{:S(2)}) collective-permute-start(f32[5,5,2,32,128]{4,3,2,1,0:T(8,128)S(1)} %slice.63.own), channel_id=1, source_target_pairs={{0,256},{1,33},{2,34},{3,259},{4,36},{5,261},{6,262},{7,39},{8,40}... | collective-permute-start | bytes 2457608 | tf_op jit(solution)/shard_map/ppermute | solution.py:69
  3.4 1.4 %fusion.12 = (f32[5,5,1,32,128]{4,3,2,1,0:T(8,128)S(1)}, f32[5,5,1,32,128]{4,3,2,1,0:T(8,128)S(1)}, f32[5,5,1,32,128]{4,3,2,1,0:T(8,128)S(1)}) fusion(f32[5,5,5,32,128]{4,3,2,1,0:T(8,128)} %bitcast.56), kind=kLoop, calls=%fused_computation.36 | loop fusion | bytes 2457600 | tf_op jit(solution)/shard_map/slice | solution.py:452
  4.8 7.7 %collective-permute-start.6 = (f32[5,5,1,32,128]{4,3,2,1,0:T(8,128)S(1)}, f32[5,5,1,32,128]{4,3,2,1,0:T(8,128)}, u32[]{:S(2)}, u32[]{:S(2)}) collective-permute-start(f32[5,5,1,32,128]{4,3,2,1,0:T(8,128)S(1)} %get-tuple-element.23.own), channel_id=1, source_target_pairs={{0,256},{1,33},{2,34},{3,259},{4,36},{5,261},{6,262},{7,39},{8,40}... | collective-permute-start | bytes 1228808 | tf_op jit(solution)/shard_map/ppermute | solution.py:69
  12.5 2.0 %collective-permute-start.4 = (f32[5,5,1,32,128]{4,3,2,1,0:T(8,128)S(1)}, f32[5,5,1,32,128]{4,3,2,1,0:T(8,128)}, u32[]{:S(2)}, u32[]{:S(2)}) collective-permute-start(f32[5,5,1,32,128]{4,3,2,1,0:T(8,128)S(1)} %get-tuple-element.24.own), channel_id=1, source_target_pairs={{0,256},{1,33},{2,34},{3,259},{4,36},{5,261},{6,262},{7,39},{8,40}... | collective-permute-start | bytes 1228808 | tf_op jit(solution)/shard_map/ppermute | solution.py:69
  14.6 7.7 %collective-permute-start = (f32[5,5,1,32,128]{4,3,2,1,0:T(8,128)S(1)}, f32[5,5,1,32,128]{4,3,2,1,0:T(8,128)S(1)}, u32[]{:S(2)}, u32[]{:S(2)}) collective-permute-start(f32[5,5,1,32,128]{4,3,2,1,0:T(8,128)S(1)} %get-tuple-element.25.own), channel_id=1, source_target_pairs={{0,256},{1,33},{2,34},{3,259},{4,36},{5,261},{6,262},{7,39},{8,40}... | collective-permute-start | bytes 1228808 | tf_op jit(solution)/shard_map/ppermute | solution.py:69
  22.4 1.0 copy.19
  23.4 0.7 fusion.1
  24.1 0.7 fusion
  24.8 1.0 reshape.190
  25.9 0.7 fusion.10
  26.6 0.1 stack.77
  26.7 0.0 copy-done.3
  26.7 0.7 fusion.5
  27.3 0.0 copy-done.1
  27.3 0.0 copy-done.2
  27.4 0.1 add_divide_fusion
  27.5 1.7 %fusion.3 = (f32[8,16,16]{2,1,0:T(8,128)S(1)}, f32[8,16,16]{2,1,0:T(8,128)S(1)}, f32[8,16,16]{2,1,0:T(8,128)S(1)}) fusion(pred[]{:T(512)S(6)} %eq.17, f32[8,16,2,16]{3,2,1,0:T(2,128)} %fusion.1, f32[8,16,2,16]{3,2,1,0:T(2,128)} %fusion), kind=kLoop, calls=%fused_computation.8 | loop fusion | flops 6144 | bytes 57345 | tf_op jit(solution)/shard_map/jit(_where)/select_n | solution.py:443
  29.2 0.1 select_n.134
  29.3 0.1 select_n.132
  29.4 0.1 select_n.138
  29.5 0.0 copy-done
  29.5 0.1 pad_add_fusion.sides
  29.6 0.0 collective-permute-done.2.got
  29.6 6.7 %piece_0.1 = (f32[5,5,2,2,2,8,128]{6,5,4,3,2,1,0:T(8,128)S(1)}, f32[5,5,2,2,4,8,128]{6,5,4,3,2,1,0:T(8,128)S(1)}) custom-call(f32[16,128]{1,0:T(8,128)S(1)} %pad_maximum_fusion.table, s32[3]{0:T(128)S(1)} %pad_add_fusion.sides, f32[5,16,128]{2,1,0:T(8,128)S(1)} %constant_dynamic-update-slice_fusion.speeds, f32[5,5,2,32,128]{4,3,2,1,0:T(8,128)S(1)} %slice.63.own, ...), custom_call_target="tpu_custom_call" | custom-call | flops 55296000 | bytes 18000000 | tf_op jit(solution)/shard_map/piece_0/pallas_call | solution.py:341
  36.3 10.9 %collective-permute-start.3 = (f32[5,5,2,2,2,8,128]{6,5,4,3,2,1,0:T(8,128)S(1)}, f32[5,5,2,2,2,8,128]{6,5,4,3,2,1,0:T(8,128)S(1)}, u32[]{:S(2)}, u32[]{:S(2)}) collective-permute-start(f32[5,5,2,2,2,8,128]{6,5,4,3,2,1,0:T(8,128)S(1)} %get-tuple-element.16), channel_id=1, source_target_pairs={{0,32},{1,257},{2,258},{3,35},{4,260},{5,37},{6,38},{7,263},{8,264... | collective-permute-start | bytes 2457608 | tf_op jit(solution)/shard_map/ppermute | solution.py:69
  47.2 0.0 collective-permute-done.6.got
  47.3 4.4 %piece_3.1 = (f32[5,5,1,2,2,8,128]{6,5,4,3,2,1,0:T(8,128)S(1)}, f32[5,5,1,2,4,8,128]{6,5,4,3,2,1,0:T(8,128)S(1)}) custom-call(f32[16,128]{1,0:T(8,128)S(1)} %pad_maximum_fusion.table, s32[3]{0:T(128)S(1)} %pad_add_fusion.sides, f32[5,16,128]{2,1,0:T(8,128)S(1)} %constant_dynamic-update-slice_fusion.speeds, f32[5,5,1,32,128]{4,3,2,1,0:T(8,128)S(1)} %get-tuple-element.23.own, ...), custom_call_target="tpu_custom_call" | custom-call | flops 27648000 | bytes 9000000 | tf_op jit(solution)/shard_map/piece_3/pallas_call | solution.py:341
  51.7 3.4 %collective-permute-start.7 = (f32[5,5,1,2,2,8,128]{6,5,4,3,2,1,0:T(8,128)S(1)}, f32[5,5,1,2,2,8,128]{6,5,4,3,2,1,0:T(8,128)S(1)}, u32[]{:S(2)}, u32[]{:S(2)}) collective-permute-start(f32[5,5,1,2,2,8,128]{6,5,4,3,2,1,0:T(8,128)S(1)} %get-tuple-element.20), channel_id=1, source_target_pairs={{0,32},{1,257},{2,258},{3,35},{4,260},{5,37},{6,38},{7,263},{8,264... | collective-permute-start | bytes 1228808 | tf_op jit(solution)/shard_map/ppermute | solution.py:69
  55.1 5.1 %collective-permute-done.4.got = f32[5,5,1,32,128]{4,3,2,1,0:T(8,128)} collective-permute-done((f32[5,5,1,32,128]{4,3,2,1,0:T(8,128)S(1)}, f32[5,5,1,32,128]{4,3,2,1,0:T(8,128)}, u32[]{:S(2)}, u32[]{:S(2)}) %collective-permute-start.4) | collective-permute-done | bytes 409632 | tf_op jit(solution)/shard_map/ppermute | solution.py:69
  60.2 4.4 %piece_2.1 = (f32[5,5,1,2,2,8,128]{6,5,4,3,2,1,0:T(8,128)S(1)}, f32[5,5,1,2,4,8,128]{6,5,4,3,2,1,0:T(8,128)S(1)}) custom-call(f32[16,128]{1,0:T(8,128)S(1)} %pad_maximum_fusion.table, s32[3]{0:T(128)S(1)} %pad_add_fusion.sides, f32[5,16,128]{2,1,0:T(8,128)S(1)} %constant_dynamic-update-slice_fusion.speeds, f32[5,5,1,32,128]{4,3,2,1,0:T(8,128)S(1)} %get-tuple-element.24.own, ...), custom_call_target="tpu_custom_call" | custom-call | flops 27648000 | bytes 9000000 | tf_op jit(solution)/shard_map/piece_2/pallas_call | solution.py:341
  64.6 12.0 %collective-permute-start.5 = (f32[5,5,1,2,2,8,128]{6,5,4,3,2,1,0:T(8,128)S(1)}, f32[5,5,1,2,2,8,128]{6,5,4,3,2,1,0:T(8,128)S(1)}, u32[]{:S(2)}, u32[]{:S(2)}) collective-permute-start(f32[5,5,1,2,2,8,128]{6,5,4,3,2,1,0:T(8,128)S(1)} %get-tuple-element.18), channel_id=1, source_target_pairs={{0,32},{1,257},{2,258},{3,35},{4,260},{5,37},{6,38},{7,263},{8,264... | collective-permute-start | bytes 1228808 | tf_op jit(solution)/shard_map/ppermute | solution.py:69
  76.7 5.3 %collective-permute-done.got = f32[5,5,1,32,128]{4,3,2,1,0:T(8,128)S(1)} collective-permute-done((f32[5,5,1,32,128]{4,3,2,1,0:T(8,128)S(1)}, f32[5,5,1,32,128]{4,3,2,1,0:T(8,128)S(1)}, u32[]{:S(2)}, u32[]{:S(2)}) %collective-permute-start) | collective-permute-done | bytes 409632 | tf_op jit(solution)/shard_map/ppermute | solution.py:69
  82.0 4.1 %piece_4.1 = (f32[5,5,1,2,2,8,128]{6,5,4,3,2,1,0:T(8,128)S(1)}, f32[5,5,1,2,4,8,128]{6,5,4,3,2,1,0:T(8,128)S(1)}) custom-call(f32[16,128]{1,0:T(8,128)S(1)} %pad_maximum_fusion.table, s32[3]{0:T(128)S(1)} %pad_add_fusion.sides, f32[5,16,128]{2,1,0:T(8,128)S(1)} %constant_dynamic-update-slice_fusion.speeds, f32[5,5,1,32,128]{4,3,2,1,0:T(8,128)S(1)} %get-tuple-element.25.own, ...), custom_call_target="tpu_custom_call" | custom-call | flops 27648000 | bytes 9000000 | tf_op jit(solution)/shard_map/piece_4/pallas_call | solution.py:341
  86.0 13.7 %collective-permute-start.1 = (f32[5,5,1,2,2,8,128]{6,5,4,3,2,1,0:T(8,128)S(1)}, f32[5,5,1,2,2,8,128]{6,5,4,3,2,1,0:T(8,128)S(1)}, u32[]{:S(2)}, u32[]{:S(2)}) collective-permute-start(f32[5,5,1,2,2,8,128]{6,5,4,3,2,1,0:T(8,128)S(1)} %get-tuple-element.14), channel_id=1, source_target_pairs={{0,32},{1,257},{2,258},{3,35},{4,260},{5,37},{6,38},{7,263},{8,264... | collective-permute-start | bytes 1228808 | tf_op jit(solution)/shard_map/ppermute | solution.py:69
  99.7 0.0 collective-permute-done.7.rest_5_
  99.8 0.0 collective-permute-done.5.rest_3_
  99.8 0.0 collective-permute-done.3.rest_1_
  99.8 1.5 %last_0.1.rest_2_ = f32[5,5,5,32,128]{4,3,2,1,0:T(8,128)} custom-call(f32[5,5,2,2,4,8,128]{6,5,4,3,2,1,0:T(8,128)S(1)} %get-tuple-element.15.rest_0_, f32[5,5,2,2,2,8,128]{6,5,4,3,2,1,0:T(8,128)S(1)} %collective-permute-done.3.rest_1_, f32[5,5,1,2,4,8,128]{6,5,4,3,2,1,0:T(8,128)S(1)} %get-tuple-element.17.rest_2_, ...), custom_call_target="tpu_custom_call" | custom-call | flops 6144000 | bytes 2000000 | tf_op jit(solution)/shard_map/last_0/pallas_call | solution.py:365
  101.3 4.6 %collective-permute-done.1.rest_1_ = f32[5,5,1,2,2,8,128]{6,5,4,3,2,1,0:T(8,128)S(1)} collective-permute-done((f32[5,5,1,2,2,8,128]{6,5,4,3,2,1,0:T(8,128)S(1)}, f32[5,5,1,2,2,8,128]{6,5,4,3,2,1,0:T(8,128)S(1)}, u32[]{:S(2)}, u32[]{:S(2)}) %collective-permute-start.1) | collective-permute-done | bytes 409632 | tf_op jit(solution)/shard_map/ppermute | solution.py:69
  105.9 0.8 last_4.1
  (14 shorter events, 0.1 us)
Async XLA Ops:
  1.2 25.4 %copy-start.3 = (f32[128]{0:T(128)S(1)}, f32[128]{0:T(128)}, u32[]{:S(2)}) copy-start(f32[128]{0:T(128)} %constant.82.clone) | copy-start | bytes 1540
  1.2 26.1 %copy-start.1 = (f32[128]{0:T(128)S(1)}, f32[128]{0:T(128)}, u32[]{:S(2)}) copy-start(f32[128]{0:T(128)} %constant.84.clone) | copy-start | bytes 1540
  1.2 26.1 %copy-start.2 = (f32[128]{0:T(128)S(1)}, f32[128]{0:T(128)}, u32[]{:S(2)}) copy-start(f32[128]{0:T(128)} %constant.83.clone) | copy-start | bytes 1540
  1.3 28.2 %copy-start = (f32[8,128]{1,0:T(8,128)S(1)}, f32[8,128]{1,0:T(8,128)}, u32[]{:S(2)}) copy-start(f32[8,128]{1,0:T(8,128)} %constant.86.clone) | copy-start | bytes 12292
  1.3 28.4 %collective-permute-start.2 = (f32[5,5,2,32,128]{4,3,2,1,0:T(8,128)S(1)}, f32[5,5,2,32,128]{4,3,2,1,0:T(8,128)S(1)}, u32[]{:S(2)}, u32[]{:S(2)}) collective-permute-start(f32[5,5,2,32,128]{4,3,2,1,0:T(8,128)S(1)} %slice.63.own), channel_id=1, source_target_pairs={{0,256},{1,33},{2,34},{3,259},{4,36},{5,261},{6,262},{7,39},{8,40}... | collective-permute-start | bytes 2457608 | tf_op jit(solution)/shard_map/ppermute | solution.py:69
  4.8 42.4 %collective-permute-start.6 = (f32[5,5,1,32,128]{4,3,2,1,0:T(8,128)S(1)}, f32[5,5,1,32,128]{4,3,2,1,0:T(8,128)}, u32[]{:S(2)}, u32[]{:S(2)}) collective-permute-start(f32[5,5,1,32,128]{4,3,2,1,0:T(8,128)S(1)} %get-tuple-element.23.own), channel_id=1, source_target_pairs={{0,256},{1,33},{2,34},{3,259},{4,36},{5,261},{6,262},{7,39},{8,40}... | collective-permute-start | bytes 1228808 | tf_op jit(solution)/shard_map/ppermute | solution.py:69
  12.5 47.7 %collective-permute-start.4 = (f32[5,5,1,32,128]{4,3,2,1,0:T(8,128)S(1)}, f32[5,5,1,32,128]{4,3,2,1,0:T(8,128)}, u32[]{:S(2)}, u32[]{:S(2)}) collective-permute-start(f32[5,5,1,32,128]{4,3,2,1,0:T(8,128)S(1)} %get-tuple-element.24.own), channel_id=1, source_target_pairs={{0,256},{1,33},{2,34},{3,259},{4,36},{5,261},{6,262},{7,39},{8,40}... | collective-permute-start | bytes 1228808 | tf_op jit(solution)/shard_map/ppermute | solution.py:69
  14.6 67.4 %collective-permute-start = (f32[5,5,1,32,128]{4,3,2,1,0:T(8,128)S(1)}, f32[5,5,1,32,128]{4,3,2,1,0:T(8,128)S(1)}, u32[]{:S(2)}, u32[]{:S(2)}) collective-permute-start(f32[5,5,1,32,128]{4,3,2,1,0:T(8,128)S(1)} %get-tuple-element.25.own), channel_id=1, source_target_pairs={{0,256},{1,33},{2,34},{3,259},{4,36},{5,261},{6,262},{7,39},{8,40}... | collective-permute-start | bytes 1228808 | tf_op jit(solution)/shard_map/ppermute | solution.py:69
  36.3 63.4 %collective-permute-start.3 = (f32[5,5,2,2,2,8,128]{6,5,4,3,2,1,0:T(8,128)S(1)}, f32[5,5,2,2,2,8,128]{6,5,4,3,2,1,0:T(8,128)S(1)}, u32[]{:S(2)}, u32[]{:S(2)}) collective-permute-start(f32[5,5,2,2,2,8,128]{6,5,4,3,2,1,0:T(8,128)S(1)} %get-tuple-element.16), channel_id=1, source_target_pairs={{0,32},{1,257},{2,258},{3,35},{4,260},{5,37},{6,38},{7,263},{8,264... | collective-permute-start | bytes 2457608 | tf_op jit(solution)/shard_map/ppermute | solution.py:69
  51.7 48.1 %collective-permute-start.7 = (f32[5,5,1,2,2,8,128]{6,5,4,3,2,1,0:T(8,128)S(1)}, f32[5,5,1,2,2,8,128]{6,5,4,3,2,1,0:T(8,128)S(1)}, u32[]{:S(2)}, u32[]{:S(2)}) collective-permute-start(f32[5,5,1,2,2,8,128]{6,5,4,3,2,1,0:T(8,128)S(1)} %get-tuple-element.20), channel_id=1, source_target_pairs={{0,32},{1,257},{2,258},{3,35},{4,260},{5,37},{6,38},{7,263},{8,264... | collective-permute-start | bytes 1228808 | tf_op jit(solution)/shard_map/ppermute | solution.py:69
  64.6 35.1 %collective-permute-start.5 = (f32[5,5,1,2,2,8,128]{6,5,4,3,2,1,0:T(8,128)S(1)}, f32[5,5,1,2,2,8,128]{6,5,4,3,2,1,0:T(8,128)S(1)}, u32[]{:S(2)}, u32[]{:S(2)}) collective-permute-start(f32[5,5,1,2,2,8,128]{6,5,4,3,2,1,0:T(8,128)S(1)} %get-tuple-element.18), channel_id=1, source_target_pairs={{0,32},{1,257},{2,258},{3,35},{4,260},{5,37},{6,38},{7,263},{8,264... | collective-permute-start | bytes 1228808 | tf_op jit(solution)/shard_map/ppermute | solution.py:69
  86.0 19.9 %collective-permute-start.1 = (f32[5,5,1,2,2,8,128]{6,5,4,3,2,1,0:T(8,128)S(1)}, f32[5,5,1,2,2,8,128]{6,5,4,3,2,1,0:T(8,128)S(1)}, u32[]{:S(2)}, u32[]{:S(2)}) collective-permute-start(f32[5,5,1,2,2,8,128]{6,5,4,3,2,1,0:T(8,128)S(1)} %get-tuple-element.14), channel_id=1, source_target_pairs={{0,32},{1,257},{2,258},{3,35},{4,260},{5,37},{6,38},{7,263},{8,264... | collective-permute-start | bytes 1228808 | tf_op jit(solution)/shard_map/ppermute | solution.py:69
